TPU v7x, 512 devices: a whole 4x4x16 slice. The times are simulated.
512 devices in a mesh: tm: 64 (over z, y), chan: 8 (over x, core).
Axes of the slice: x: 4, y: 4, z: 16, core: 2. Of those that a mesh axis runs over, the one named last changes fastest.
Arguments:
- signal: bfloat16 [304, 131072], P('chan', 'tm'), may hold values from -160 to 160
- filters: bfloat16 [304, 64, 256], P('chan'), may hold values from -0.0390625 to 0.0390625
Outputs:
- basis: float32 [131072, 256], P(('tm', 'chan'))
All inputs are finite; a program needn't handle non-finite values.
Results may differ from a plain program's by a relative error of at most 0.0003.
Values may be sent and summed in bfloat16 or wider, within the bound.
A program may use at most 64 MiB of HBM per device.

v0:
```python
import math

import jax
import jax.numpy as jnp
from jax import lax
from jax.sharding import Mesh
from jax.sharding import PartitionSpec as P

CHAN = ("chan_0", "chan_1")
TM = ("tm_0", "tm_1")
TM_CHAN = ("tm_0", "tm_1", "chan_0", "chan_1")


def passed_along(block, axis, distance):
    devices = range(lax.axis_size(axis))
    route = [(i - distance, i) for i in devices if i - distance in devices]
    return lax.ppermute(block, axis, route)


def cut_along(x, dim, length):
    before, after = (x.shape[:dim], x.shape[dim + 1 :])
    return jnp.moveaxis(x.reshape(*before, length, -1, *after), dim, 0)


def sum_at_owner(x, axis, dim):
    blocks = cut_along(x, dim, lax.axis_size(axis))
    arrived = lax.all_to_all(blocks, axis, split_axis=0, concat_axis=0, tiled=True)
    return arrived.sum(axis=0)


def filled_up(lines, length):
    spare = -len(lines) % length
    return jnp.pad(lines, [(0, spare)] + [(0, 0)] * (lines.ndim - 1))


def from_everyone(x, axis):
    copies = jnp.broadcast_to(x, (lax.axis_size(axis), *x.shape))
    return lax.all_to_all(copies, axis, split_axis=0, concat_axis=0, tiled=True)


def joined_along(blocks, dim):
    blocks = jnp.moveaxis(blocks, 0, dim)
    shape = blocks.shape
    return blocks.reshape(*shape[:dim], shape[dim] * shape[dim + 1], *shape[dim + 2 :])


def whole_of(x, axes, dim):
    far, near = axes
    blocks = from_everyone(from_everyone(x, far), near)
    return joined_along(blocks.swapaxes(0, 1).reshape(-1, *x.shape), dim)


def sum_by_axis(x, axes, dim):
    far, near = axes
    own = sum_at_owner(cut_along(x, dim, lax.axis_size(far)), near, dim + 1)
    return jnp.sum(lax.all_to_all(own, far, 0, 0, tiled=True), axis=0)


def nested_sum(x, axes):
    lines = x.reshape(-1)
    padded = filled_up(lines, lax.axis_size(axes[0]) * lax.axis_size(axes[1]))
    whole = whole_of(sum_by_axis(padded, axes, 0), axes, 0)
    return lax.slice_in_dim(whole, 0, len(lines)).reshape(x.shape)


def lag_projection(extended, filters):
    result = lax.conv_general_dilated(
        extended[None],
        filters,
        (1,),
        "VALID",
        dimension_numbers=("NCH", "IHO", "NHC"),
        preferred_element_type=jnp.float32,
    )
    return result[0]


def partial_gram_matrix(input_series):
    return lax.dot_general(
        input_series,
        input_series,
        (((0,), (0,)), ((), ())),
        precision=lax.Precision.HIGHEST,
        preferred_element_type=jnp.float32,
    )


def per_device(signal, filters):
    lag_count = filters.shape[1]
    shard_len = signal.shape[1]
    sample_count = shard_len * lax.axis_size(TM)
    leading_basis = signal[:, : lag_count - 1]
    following = passed_along(leading_basis, TM, -1)
    extended = jnp.concatenate([signal, following], axis=1)
    own_rows = sum_at_owner(lag_projection(extended, filters), CHAN, 0)
    gram_sum = nested_sum(partial_gram_matrix(own_rows), (("tm_0", "tm_1"), ("chan_0", "chan_1")))
    lower_factor = jnp.linalg.cholesky(gram_sum)
    solved = lax.linalg.triangular_solve(
        lower_factor, own_rows, left_side=False, lower=True, transpose_a=True
    )
    return solved * math.sqrt(sample_count)


def solution(mesh):
    torus = Mesh(mesh.devices.reshape(16, 4, 4, 2), ("tm_0", "tm_1", "chan_0", "chan_1"))
    placed = (P(CHAN, TM), P(CHAN, None, None))
    return jax.shard_map(
        per_device, mesh=torus, in_specs=placed, out_specs=P(TM_CHAN, None), check_vma=False
    )
```

profile of v0, /device:TPU:1, one launch (start us, length us, event | category | flops | bytes accessed | tf_op | source)
XLA Modules:
  0.0 199.4 jit_solution(10822091385823367925)
XLA Ops:
  0.0 0.8 slice.45
  0.8 1.3 collective-permute-start
  2.1 3.8 %collective-permute-done = bf16[38,63]{1,0:T(8,128)(2,1)S(1)} collective-permute-done((bf16[38,63]{1,0:T(8,128)(2,1)S(1)}, bf16[38,63]{1,0:T(8,128)(2,1)S(1)}, u32[]{:S(2)}, u32[]{:S(2)}) %collective-permute-start) | collective-permute-done | bytes 4820 | tf_op jit(solution)/shard_map/ppermute | solution.py:17
  5.9 0.9 maximum_bitcast_fusion
  6.8 1.6 copy.12
  8.4 18.2 %fusion = f32[1,2048,256]{2,0,1:T(1,128)S(1)} fusion(bf16[1,38,2111]{1,0,2:T(2,128)(2,1)S(1)} %copy.12, bf16[38,64,256]{2,1,0:T(8,128)(2,1)S(1)} %copy-done), kind=kOutput, calls=%fused_computation.2 | convolution fusion | flops 2550136832 | bytes 3502772 | tf_op jit(solution)/shard_map/conv_general_dilated | solution.py:67
  26.8 36.3 %all_to_all.33 = f32[8,256,256]{2,1,0:T(8,128)S(1)} all-to-all(f32[8,256,256]{2,1,0:T(8,128)S(1)} %bitcast.43), channel_id=1, replica_groups=mesh['tm_0'=16,'tm_1'=4,'chan_0'=4,'chan_1'=2] {'chan_0','chan_1'}, dimensions={0} | all-to-all | bytes 4194304 | tf_op jit(solution)/shard_map/all_to_all | solution.py:27
  63.1 0.8 reduce_sum.27
  63.9 1.6 fusion.11
  65.6 9.9 %all_to_all.34 = f32[8,64,128]{2,1,0:T(8,128)S(1)} all-to-all(f32[8,64,128]{2,1,0:T(8,128)S(1)} %bitcast.45), channel_id=1, replica_groups=mesh['tm_0'=16,'tm_1'=4,'chan_0'=4,'chan_1'=2] {'chan_0','chan_1'}, dimensions={0} | all-to-all | bytes 524288 | tf_op jit(solution)/shard_map/all_to_all | solution.py:27
  75.6 29.9 %all_to_all.35 = f32[64,1,128]{2,1,0:T(1,128)S(1)} all-to-all(f32[64,1,128]{2,1,0:T(1,128)S(1)} %bitcast.46), channel_id=1, replica_groups=mesh['tm_0'=16,'tm_1'=4,'chan_0'=4,'chan_1'=2] {'tm_0','tm_1'}, dimensions={0} | all-to-all | bytes 65536 | tf_op jit(solution)/shard_map/all_to_all | solution.py:56
  105.6 17.4 %all_to_all.36 = f32[64,1,128]{2,1,0:T(1,128)S(1)} all-to-all(f32[64,1,128]{2,1,0:T(1,128)S(1)} %broadcast_in_dim.12), channel_id=1, replica_groups=mesh['tm_0'=16,'tm_1'=4,'chan_0'=4,'chan_1'=2] {'tm_0','tm_1'}, dimensions={0} | all-to-all | bytes 65536 | tf_op jit(solution)/shard_map/all_to_all | solution.py:38
  123.0 0.7 broadcast_in_dim.13
  123.7 6.9 %all-to-all-start.4 = ((f32[8,64,128]{2,1,0:T(8,128)}), f32[8,64,128]{2,1,0:T(8,128)S(1)}, u32[]{:S(2)}, u32[]{:S(2)}) async-start(f32[8,64,128]{2,1,0:T(8,128)} %broadcast_in_dim.13), calls=%async_computation.4 | async-start | bytes 524288 | tf_op jit(solution)/shard_map/all_to_all | solution.py:38
  130.6 6.5 %all-to-all-done.4 = f32[8,64,128]{2,1,0:T(8,128)S(1)} async-done(((f32[8,64,128]{2,1,0:T(8,128)}), f32[8,64,128]{2,1,0:T(8,128)S(1)}, u32[]{:S(2)}, u32[]{:S(2)}) %all-to-all-start.4) | async-done | bytes 262176 | tf_op jit(solution)/shard_map/all_to_all | solution.py:38
  137.1 0.2 copy.15
  137.6 11.7 %cholesky.50 = f32[128,128]{1,0:T(8,128)S(1)} custom-call(f32[128,128]{1,0:T(8,128)S(1)} %cholesky.118), custom_call_target="Cholesky" | custom-call | tf_op jit(solution)/shard_map/jit(cholesky)/cholesky | solution.py:97
  149.4 9.8 %custom-call.14 = f32[1,128,128]{1,2,0:T(8,128)S(1)} custom-call(f32[1,128,128]{2,1,0:T(8,128)S(1)} %get-tuple-element.26), custom_call_target="InvertDiagBlocksLowerTriangular" | custom-call | tf_op jit(solution)/shard_map/jit(cholesky)/cholesky | solution.py:97
  159.2 0.2 constant_dynamic-update-slice_fusion.1
  159.4 0.3 convolution_subtract_fusion.1
  159.7 11.7 %cholesky.105 = f32[128,128]{1,0:T(8,128)S(1)} custom-call(f32[128,128]{1,0:T(8,128)S(1)} %convolution_subtract_fusion.1), custom_call_target="Cholesky" | custom-call | tf_op jit(solution)/shard_map/jit(cholesky)/cholesky | solution.py:97
  171.4 0.7 compare_reduce_fusion
  173.5 4.1 %while.1 = (s32[]{:T(128)}, f32[256,256]{1,0:T(8,128)S(1)}, s32[2,2]{1,0:T(2,128)S(1)}, f32[2,128,128]{2,1,0:T(8,128)S(1)}, s32[]{:T(128)}) while((s32[]{:T(128)}, f32[256,256]{1,0:T(8,128)S(1)}, s32[2,2]{1,0:T(2,128)S(1)}, f32[2,128,128]{2,1,0:T(8,128)S(1)}, s32[]{:T(128)}) %tuple.23), condition=%wide.while_cond, body=%wide.while_body.sunk | while | flops 2 | bytes 131181 | solution.py:98
  173.5 0.7 fusion.20
  174.2 1.3 bitcast_dynamic-update-slice_fusion.2
  175.5 0.7 fusion.20
  176.2 1.3 bitcast_dynamic-update-slice_fusion.2
  177.6 19.9 %custom-call.15 = f32[2,128,128]{1,2,0:T(8,128)S(1)} custom-call(f32[2,128,128]{2,1,0:T(8,128)S(1)} %get-tuple-element.12), custom_call_target="InvertDiagBlocksLowerTriangular" | custom-call | tf_op jit(solution)/shard_map/triangular_solve | solution.py:98
  197.5 0.3 fusion.3
  197.8 0.4 convolution_subtract_fusion
  198.2 0.3 fusion.5
  198.5 0.8 copy.17
  (24 shorter events, 0.8 us)
Async XLA Ops:
  0.0 8.4 %copy-start = (bf16[38,64,256]{2,1,0:T(8,128)(2,1)S(1)}, bf16[38,64,256]{2,1,0:T(8,128)(2,1)}, u32[]{:S(2)}) copy-start(bf16[38,64,256]{2,1,0:T(8,128)(2,1)} %param.3) | copy-start | bytes 3735556
  0.8 5.1 %collective-permute-start = (bf16[38,63]{1,0:T(8,128)(2,1)S(1)}, bf16[38,63]{1,0:T(8,128)(2,1)S(1)}, u32[]{:S(2)}, u32[]{:S(2)}) collective-permute-start(bf16[38,63]{1,0:T(8,128)(2,1)S(1)} %slice.45), channel_id=1, source_target_pairs={{8,0},{16,8},{24,16},{32,24},{40,32},{48,40},{56,48},{64,56},{72,6... | collective-permute-start | bytes 14372 | tf_op jit(solution)/shard_map/ppermute | solution.py:17
  123.7 13.5 %all-to-all-start.4 = ((f32[8,64,128]{2,1,0:T(8,128)}), f32[8,64,128]{2,1,0:T(8,128)S(1)}, u32[]{:S(2)}, u32[]{:S(2)}) async-start(f32[8,64,128]{2,1,0:T(8,128)} %broadcast_in_dim.13), calls=%async_computation.4 | async-start | bytes 524288 | tf_op jit(solution)/shard_map/all_to_all | solution.py:38
  149.3 48.2 %copy-start.1 = (f32[256,256]{1,0:T(8,128)S(1)}, f32[256,256]{1,0:T(8,128)}, u32[]{:S(2)}) copy-start(f32[256,256]{1,0:T(8,128)} %reduce_sum.27) | copy-start | bytes 786436
where the time goes:
time: 200 us; the launch traced here: 199 us
  blocking collectives  93.5 us (47%)
  other arithmetic  55.9 us (28%)
  matrix products  21.3 us (11%)
  waiting for transfers between devices  10.3 us (5%)
  local copies, waits for them, and re-layouts  8.68 us (4%)
  starting transfers between devices  8.21 us (4%)
    all_to_all x2, blocking collectives, sum_at_owner(): lax.all_to_all(blocks, axis, split_axis=0, concat_axis=0, tiled=True)  46.2 us
    another operation x6, other arithmetic, per_device(): lower_factor = jnp.linalg.cholesky(gram_sum)  34 us
    all_to_all x1, blocking collectives, sum_by_axis(): return jnp.sum(lax.all_to_all(own, far, 0, 0, tiled=True), axis=0)  29.9 us
    another operation x3, other arithmetic, per_device(): lax.linalg.triangular_solve(lower_factor, own_rows, left_side=False, lowe...  19.9 us
    conv_general_dilated x1, matrix products, lag_projection(): lax.conv_general_dilated(extended[None], filters, (1,), 'VALID', dimensio...  18.2 us
    all_to_all x1, blocking collectives, from_everyone(): return lax.all_to_all(copies, axis, split_axis=0, concat_axis=0, tiled=True)  17.4 us
    all_to_all x1, starting transfers between devices, from_everyone(): return lax.all_to_all(copies, axis, split_axis=0, concat_axis=0, tiled=True)  6.93 us
    all_to_all x1, waiting for transfers between devices, from_everyone(): return lax.all_to_all(copies, axis, split_axis=0, concat_axis=0, tiled=True)  6.52 us
  transfers between devices with their start and end apart: 2, of which 2 were waited for; matrix products, arithmetic and copies ran while one was open for 0% of the time, Pallas kernels for 0%

commit v1 on v0

v1 whole, which is shorter than its diff:
```python
import functools
import math

import jax
import jax.numpy as jnp
from jax import lax
from jax.experimental import pallas as pl
from jax.experimental.pallas import tpu as pltpu
from jax.sharding import Mesh
from jax.sharding import PartitionSpec as P

AXES = ("z", "y", "x", "core")
CHAN = ("x", "core")
TM = ("z", "y")
MESH = pl.DeviceIdType.MESH
HIGHEST = lax.Precision.HIGHEST
WIDTH = 128


def reversed_and_turned(filters, turned, lags):
    count = filters.shape[0]
    row = lax.broadcasted_iota(jnp.int32, (256, 256), 0)
    column = lax.broadcasted_iota(jnp.int32, (256, 256), 1)
    flip = jnp.where(row + column == 2 * lags * (row // lags) + lags - 1, 1.0, 0.0)
    flip = flip.astype(jnp.bfloat16)
    for first in range(0, count, 256):
        n = min(256, count - first)
        block = jnp.dot(
            flip[:n, :n], filters[first : first + n, :], preferred_element_type=jnp.float32
        )
        turned[:, first : first + n] = block.T.astype(jnp.bfloat16)


def lagged(wide, hankel, lags, sensors, start, width):
    row = lax.broadcasted_iota(jnp.int32, (lags, WIDTH), 0)
    lane = lax.broadcasted_iota(jnp.int32, (lags, WIDTH), 1)
    first = WIDTH - lags + 1
    inside = lane < first + row
    tiles = width // WIDTH
    for c in range(sensors):
        turned = []
        for j in range(tiles + 1):
            line = wide[c : c + 1, pl.ds(pl.multiple_of(start + WIDTH * j, WIDTH), WIDTH)]
            line = jnp.broadcast_to(line, (lags, WIDTH))
            turned.append(pltpu.roll(line, first, 1, stride=1, stride_axis=0))
        for j in range(tiles):
            tile = jnp.where(inside, turned[j], turned[j + 1])
            hankel[c * lags : (c + 1) * lags, WIDTH * j : WIDTH * (j + 1)] = tile.astype(
                jnp.bfloat16
            )


def project_and_sum(
    sizes, lags, signal, filters, series_out, gram_out,
    wide, turned, hankel, edge, parts, from_core, to_chips, from_chips,
    gram, scattered, shard, from_line,
    edge_send, edge_recv, core_send, core_recv, chip_send, chip_recv,
    scatter_send, scatter_recv, line_send, line_recv, gather_send, gather_recv,
):
    nz, ny, nx, nc = sizes
    z, y, x, core = (lax.axis_index(a) for a in AXES)
    sensors, length = signal.shape
    rank = z * ny + y
    shards = nz * ny
    before = lax.rem(rank + shards - 1, shards)
    after = lax.rem(rank + 1, shards)

    def plane(dy, dx, dc):
        return (z, lax.rem(y + dy, ny), lax.rem(x + dx, nx), lax.rem(core + dc, nc))

    steps = [(dy, dx, dc) for dy in range(ny) for dx in range(nx) for dc in range(nc)][1:]
    neighbours = [plane(*s) for s in steps]
    line = [(lax.rem(z + d, nz), y, x, core) for d in range(1, nz)]
    behind = (before // ny, lax.rem(before, ny), x, core)
    ahead = (after // ny, lax.rem(after, ny), x, core)

    barrier = pltpu.get_barrier_semaphore()
    everyone = neighbours + line + [behind, ahead]
    for device in everyone:
        pl.semaphore_signal(barrier, inc=1, device_id=device, device_id_type=MESH)

    wide[:sensors, :length] = signal[...].astype(jnp.float32)
    edge[0, :sensors, :] = signal[:, :WIDTH]
    reversed_and_turned(filters, turned, lags)
    pl.semaphore_wait(barrier, len(everyone))

    edge_copy = pltpu.make_async_remote_copy(
        edge.at[0], edge.at[1], edge_send, edge_recv, device_id=behind, device_id_type=MESH
    )
    edge_copy.start()
    edge_copy.wait()
    following = edge[1, :sensors, :].astype(jnp.float32)
    wide[:sensors, length:] = jnp.where(rank == shards - 1, jnp.zeros_like(following), following)

    rows = from_core.shape[2]
    partner = plane(0, 0, 1)
    other = 1 - core

    def to_core(i):
        return pltpu.make_async_remote_copy(
            parts.at[i, other], from_core.at[i], core_send.at[i], core_recv.at[i],
            device_id=partner, device_id_type=MESH,
        )

    def distance(i):
        return jnp.where(i == 0, 2, jnp.where(i == 1, 1, jnp.where(i == 2, 3, 0)))

    def to_chip(i):
        return pltpu.make_async_remote_copy(
            to_chips.at[i], from_chips.at[i], chip_send.at[i], chip_recv.at[i],
            device_id=plane(0, distance(i), 0), device_id_type=MESH,
        )

    def pass_on(i):
        to_core(i).wait_recv()
        to_chips[i] = parts[i, core] + from_core[i]
        to_chip(i).start()

    def step(i, carry):
        chip = lax.rem(x + distance(i), nx)
        lagged(wide, hankel, lags, sensors, chip * (2 * rows), 2 * rows)
        part = jnp.dot(turned[...], hankel[...], preferred_element_type=jnp.float32)
        parts[i, 0] = part[:, :rows]
        parts[i, 1] = part[:, rows:]
        to_core(i).start()

        @pl.when(i > 0)
        def _():
            pass_on(i - 1)

        return carry

    lax.fori_loop(0, nx, step, 0)
    to_core(nx - 1).wait_recv()
    own = parts[nx - 1, core] + from_core[nx - 1]
    for i in range(nx - 1):
        to_chip(i).wait_recv()
        own = own + from_chips[i]
    series_out[...] = own
    gram[...] = lax.dot_general(
        own, own, (((1,), (1,)), ((), ())), precision=HIGHEST, preferred_element_type=jnp.float32
    )

    height = shard.shape[0]

    def place(dy, dx, dc):
        _, py, px, pc = plane(dy, dx, dc)
        index = (py * nx + px) * nc + pc
        return pl.ds(pl.multiple_of(index * height, height), height)

    scatters = [
        pltpu.make_async_remote_copy(
            gram.at[place(*s)], scattered.at[n], scatter_send.at[n], scatter_recv.at[n],
            device_id=neighbours[n], device_id_type=MESH,
        )
        for n, s in enumerate(steps)
    ]
    for copy in scatters:
        copy.start()
    mine = place(0, 0, 0)
    total = gram[mine]
    for n, copy in enumerate(scatters):
        copy.wait_recv()
        total = total + scattered[n]
    shard[...] = total

    lines = [
        pltpu.make_async_remote_copy(
            shard, from_line.at[n], line_send.at[n], line_recv.at[n],
            device_id=device, device_id_type=MESH,
        )
        for n, device in enumerate(line)
    ]
    for copy in lines:
        copy.start()
    for n, copy in enumerate(lines):
        copy.wait_recv()
        total = total + from_line[n]
    gram_out[mine] = total

    gathers = [
        pltpu.make_async_remote_copy(
            gram_out.at[mine], gram_out.at[mine], gather_send.at[n], gather_recv.at[n],
            device_id=neighbours[n], device_id_type=MESH,
        )
        for n in range(len(steps))
    ]
    for copy in gathers:
        copy.start()
    for copy in gathers:
        copy.wait_recv()

    edge_done = [to_core(i) for i in range(nx)] + [to_chip(i) for i in range(nx - 1)]
    for copy in edge_done + scatters + lines + gathers:
        copy.wait_send()


def per_device(sizes, signal, filters):
    nz, ny, nx, nc = sizes
    sensors, length = signal.shape
    _, lags, depth = filters.shape
    rows = length // (nx * nc)
    group = ny * nx * nc
    height = depth // group
    high = -(-sensors // 16) * 16
    vmem = pl.BlockSpec(memory_space=pltpu.VMEM)
    f32, bf16 = jnp.float32, jnp.bfloat16
    dma = pltpu.SemaphoreType.DMA
    series, gram = pl.pallas_call(
        functools.partial(project_and_sum, sizes, lags),
        out_shape=(
            jax.ShapeDtypeStruct((depth, rows), f32),
            jax.ShapeDtypeStruct((depth, depth), f32),
        ),
        in_specs=[vmem, vmem],
        out_specs=(vmem, vmem),
        scratch_shapes=[
            pltpu.VMEM((high, length + WIDTH), f32),
            pltpu.VMEM((depth, sensors * lags), bf16),
            pltpu.VMEM((sensors * lags, 2 * rows), bf16),
            pltpu.VMEM((2, high, WIDTH), bf16),
            pltpu.VMEM((nx, nc, depth, rows), f32),
            pltpu.VMEM((nx, depth, rows), f32),
            pltpu.VMEM((nx - 1, depth, rows), f32),
            pltpu.VMEM((nx - 1, depth, rows), f32),
            pltpu.VMEM((depth, depth), f32),
            pltpu.VMEM((group - 1, height, depth), f32),
            pltpu.VMEM((height, depth), f32),
            pltpu.VMEM((nz - 1, height, depth), f32),
            dma, dma, dma((nx,)), dma((nx,)), dma((nx - 1,)), dma((nx - 1,)),
            dma((group - 1,)), dma((group - 1,)), dma((nz - 1,)), dma((nz - 1,)),
            dma((group - 1,)), dma((group - 1,)),
        ],
        compiler_params=pltpu.CompilerParams(
            collective_id=0, has_side_effects=True, vmem_limit_bytes=48 << 20
        ),
        name="project_and_sum",
    )(signal, filters.reshape(sensors * lags, depth))
    sample_count = length * nz * ny
    lower = jnp.linalg.cholesky(gram)
    solved = lax.linalg.triangular_solve(
        lower, series.T, left_side=False, lower=True, transpose_a=True
    )
    return solved * math.sqrt(sample_count)


def solution(mesh):
    sizes = (16, 4, 4, 2)
    torus = Mesh(mesh.devices.reshape(sizes), AXES)
    return jax.shard_map(
        functools.partial(per_device, sizes),
        mesh=torus,
        in_specs=(P(CHAN, TM), P(CHAN, None, None)),
        out_specs=P(TM + CHAN, None),
        check_vma=False,
    )
```

time: 200 us -> 125 us (0.62)
  blocking collectives: 93.5 us -> 0 us
  Pallas kernels: 0 us -> 60.2 us
  matrix products: 21.3 us -> 1.38 us
  waiting for transfers between devices: 10.3 us -> 0 us
  starting transfers between devices: 8.21 us -> 0 us
    all_to_all x4 -> x0, blocking collectives: 93.5 us -> none  [the longest x2 46.2 us: sum_at_owner(): lax.all_to_all(blocks, axis, split_axis=0, concat_axis=0, tiled=True)]
    pallas_call x0 -> x1, Pallas kernels: none -> 60.2 us  [per_device(): pl.pallas_call(functools.partial(project_and_sum, sizes, lags), out_shape...]
    conv_general_dilated x1 -> x0, matrix products: 18.2 us -> none  [lag_projection(): lax.conv_general_dilated(extended[None], filters, (1,), 'VALID', dimensio...]
    all_to_all x1 -> x0, starting transfers between devices: 6.93 us -> none  [from_everyone(): return lax.all_to_all(copies, axis, split_axis=0, concat_axis=0, tiled=True)]
    all_to_all x1 -> x0, waiting for transfers between devices: 6.52 us -> none  [from_everyone(): return lax.all_to_all(copies, axis, split_axis=0, concat_axis=0, tiled=True)]
    ppermute x1 -> x0, waiting for transfers between devices: 3.79 us -> none  [passed_along(): return lax.ppermute(block, axis, route)]
    broadcast_in_dim x3 -> x0, local copies, waits for them, and re-layouts: 2.34 us -> none  [the longest x1 1.61 us: lag_projection(): extended[None]]
    unnamed x5 -> x4, local copies, waits for them, and re-layouts: 0.15 us -> 2.21 us
  transfers between devices with their start and end apart: 2 -> 0, of which waited for: 2 -> 0; matrix products, arithmetic and copies ran while one was open for 0% -> 0% of each run, Pallas kernels for 0% -> 0%
where the time goes in v1:
time: 125 us; the launch traced here: 124 us
  Pallas kernels  60.2 us (48%)
  other arithmetic  54 us (43%)
  local copies, waits for them, and re-layouts  7.29 us (6%)
  between operations  1.47 us (1%)
  matrix products  1.38 us (1%)
    pallas_call x1, Pallas kernels, per_device(): pl.pallas_call(functools.partial(project_and_sum, sizes, lags), out_shape...  60.2 us
    another operation x6, other arithmetic, per_device(): lower = jnp.linalg.cholesky(gram)  34 us
    another operation x3, other arithmetic, per_device(): lax.linalg.triangular_solve(lower, series.T, left_side=False, lower=True,...  19.9 us
    another operation x6, local copies, waits for them, and re-layouts  4.02 us

profile of v1, /device:TPU:1, one launch (start us, length us, event | category | flops | bytes accessed | tf_op | source)
XLA Modules:
  0.0 124.3 jit_solution(15685672710978101338)
XLA Ops:
  0.0 0.0 copy-start
  0.0 1.3 %copy-done = bf16[38,64,256]{2,1,0:T(8,128)(2,1)S(1)} copy-done((bf16[38,64,256]{2,1,0:T(8,128)(2,1)S(1)}, bf16[38,64,256]{2,1,0:T(8,128)(2,1)}, u32[]{:S(2)}) %copy-start) | copy-done | bytes 1245208
  1.3 0.0 copy-start.1
  1.3 0.9 copy-done.1
  2.2 60.2 %project_and_sum.1 = (f32[256,256]{1,0:T(8,128)S(1)}, f32[256,256]{1,0:T(8,128)S(1)}) custom-call(bf16[38,2048]{1,0:T(8,128)(2,1)S(1)} %copy-done.1, bf16[2432,256]{1,0:T(8,128)(2,1)S(1)} %bitcast.33), custom_call_target="tpu_custom_call" | custom-call | tf_op jit(solution)/shard_map/project_and_sum/pallas_call | solution.py:209
  62.4 0.1 copy.3
  62.6 11.7 %cholesky.50 = f32[128,128]{1,0:T(8,128)S(1)} custom-call(f32[128,128]{1,0:T(8,128)S(1)} %cholesky.118), custom_call_target="Cholesky" | custom-call | tf_op jit(solution)/shard_map/jit(cholesky)/cholesky | solution.py:240
  74.3 9.8 %custom-call.14 = f32[1,128,128]{1,2,0:T(8,128)S(1)} custom-call(f32[1,128,128]{2,1,0:T(8,128)S(1)} %get-tuple-element.30), custom_call_target="InvertDiagBlocksLowerTriangular" | custom-call | tf_op jit(solution)/shard_map/jit(cholesky)/cholesky | solution.py:240
  84.2 0.2 constant_dynamic-update-slice_fusion.1
  84.4 0.3 convolution_subtract_fusion.1
  84.7 11.7 %cholesky.105 = f32[128,128]{1,0:T(8,128)S(1)} custom-call(f32[128,128]{1,0:T(8,128)S(1)} %convolution_subtract_fusion.1), custom_call_target="Cholesky" | custom-call | tf_op jit(solution)/shard_map/jit(cholesky)/cholesky | solution.py:240
  96.4 0.7 compare_reduce_fusion
  98.5 0.1 triangular_solve.58
  98.6 4.1 %while.1 = (s32[]{:T(128)}, f32[256,256]{1,0:T(8,128)S(1)}, s32[2,2]{1,0:T(2,128)S(1)}, f32[2,128,128]{2,1,0:T(8,128)S(1)}, s32[]{:T(128)}) while((s32[]{:T(128)}, f32[256,256]{1,0:T(8,128)S(1)}, s32[2,2]{1,0:T(2,128)S(1)}, f32[2,128,128]{2,1,0:T(8,128)S(1)}, s32[]{:T(128)}) %tuple.23), condition=%wide.while_cond, body=%wide.while_body.sunk | while | flops 2 | bytes 131181 | solution.py:241
  98.6 0.7 fusion.14
  99.3 1.3 %bitcast_dynamic-update-slice_fusion.2 = f32[2,128,128]{2,1,0:T(8,128)S(1)} fusion(f32[2,128,128]{2,1,0:T(8,128)S(1)} %get-tuple-element.72, s32[]{:T(128)} %get-tuple-element.69, f32[256,256]{1,0:T(8,128)S(1)} %get-tuple-element.75, s32[]{:T(128)} %bitcast.31, s32[]{:T(128)} %bitcast.32), kind=kLoop, calls=%fused_computation.clone.1 | loop fusion | bytes 131084 | tf_op jit(solution)/shard_map/triangular_solve
  100.7 0.7 fusion.14
  101.3 1.3 %bitcast_dynamic-update-slice_fusion.2 = f32[2,128,128]{2,1,0:T(8,128)S(1)} fusion(f32[2,128,128]{2,1,0:T(8,128)S(1)} %get-tuple-element.72, s32[]{:T(128)} %get-tuple-element.69, f32[256,256]{1,0:T(8,128)S(1)} %get-tuple-element.75, s32[]{:T(128)} %bitcast.31, s32[]{:T(128)} %bitcast.32), kind=kLoop, calls=%fused_computation.clone.1 | loop fusion | bytes 131084 | tf_op jit(solution)/shard_map/triangular_solve
  102.7 19.9 %custom-call.15 = f32[2,128,128]{1,2,0:T(8,128)S(1)} custom-call(f32[2,128,128]{2,1,0:T(8,128)S(1)} %get-tuple-element.16), custom_call_target="InvertDiagBlocksLowerTriangular" | custom-call | tf_op jit(solution)/shard_map/triangular_solve | solution.py:241
  122.5 0.3 fusion.1
  122.9 0.3 convolution_subtract_fusion
  123.2 0.3 fusion.3
  123.5 0.8 copy.4
  (11 shorter events, 0.2 us)
Async XLA Ops:
  0.0 1.3 %copy-start = (bf16[38,64,256]{2,1,0:T(8,128)(2,1)S(1)}, bf16[38,64,256]{2,1,0:T(8,128)(2,1)}, u32[]{:S(2)}) copy-start(bf16[38,64,256]{2,1,0:T(8,128)(2,1)} %param.3) | copy-start | bytes 3735556
  1.3 0.9 copy-start.1

commit v2 on v1

--- a/solution.py
+++ b/solution.py
@@ -193,6 +193,97 @@
     edge_done = [to_core(i) for i in range(nx)] + [to_chip(i) for i in range(nx - 1)]
     for copy in edge_done + scatters + lines + gathers:
         copy.wait_send()
+
+
+NN = ((1,), (0,))
+NT = ((1,), (1,))
+
+
+def dot(a, b, dims):
+    return lax.dot_general(
+        a, b, (dims, ((), ())), precision=HIGHEST, preferred_element_type=jnp.float32
+    )
+
+
+def spread(x):
+    return jnp.broadcast_to(x, (8, WIDTH))
+
+
+def refined_reciprocal(x):
+    r = pltpu.reciprocal(x, approx=True)
+    return r * (2.0 - x * r)
+
+
+def inverse_factor(tiles, q=8):
+    count = len(tiles)
+    sub = lax.broadcasted_iota(jnp.int32, (8, WIDTH), 0)
+    lane = lax.broadcasted_iota(jnp.int32, (8, WIDTH), 1)
+    left = list(tiles)
+    right = [jnp.where(lane == sub + 8 * g, 1.0, 0.0) for g in range(count)]
+    inverse = [jnp.zeros((8, WIDTH), jnp.float32)] * count
+    for j in range(0, 8 * count, q):
+        g, s = divmod(j, 8)
+        rl = [spread(left[g][s + i : s + i + 1, :]) for i in range(q)]
+        rr = [spread(right[g][s + i : s + i + 1, :]) for i in range(q)]
+        e = {(i, k): spread(rl[i][:, j + k : j + k + 1]) for i in range(q) for k in range(i, q)}
+        wl, wr, v = [None] * q, [None] * q, {}
+        for i in range(0, q, 2):
+            a, b, c = e[i, i], e[i, i + 1], e[i + 1, i + 1]
+            inv = refined_reciprocal(a * c - b * b)
+            ci, bi, ai = c * inv, b * inv, a * inv
+            for k in range(i + 2, q):
+                v[i, k] = ci * e[i, k] - bi * e[i + 1, k]
+                v[i + 1, k] = ai * e[i + 1, k] - bi * e[i, k]
+            for k in range(i + 2, q):
+                for m in range(k, q):
+                    e[k, m] = e[k, m] - (e[i, k] * v[i, m] + e[i + 1, k] * v[i + 1, m])
+            wl[i], wl[i + 1] = ci * rl[i] - bi * rl[i + 1], ai * rl[i + 1] - bi * rl[i]
+            wr[i], wr[i + 1] = ci * rr[i] - bi * rr[i + 1], ai * rr[i + 1] - bi * rr[i]
+            for k in range(i + 2, q):
+                rl[k] = rl[k] - (e[i, k] * wl[i] + e[i + 1, k] * wl[i + 1])
+                rr[k] = rr[k] - (e[i, k] * wr[i] + e[i + 1, k] * wr[i + 1])
+            root_a = lax.rsqrt(a)
+            ratio = b * (root_a * root_a)
+            root_c = lax.rsqrt(c - b * ratio)
+            first = rr[i] * root_a
+            second = (rr[i + 1] - ratio * rr[i]) * root_c
+            inverse[g] = jnp.where(
+                sub == s + i, first, jnp.where(sub == s + i + 1, second, inverse[g])
+            )
+        for h in range(g, count):
+            if h == g and s + q == 8:
+                continue
+            m = [spread(left[h][:, j + k : j + k + 1]) for k in range(q)]
+            for i in range(0, q, 2):
+                for k in range(i + 2, q):
+                    m[k] = m[k] - (m[i] * v[i, k] + m[i + 1] * v[i + 1, k])
+            if h == g:
+                m = [jnp.where(sub >= s + q, x, 0.0) for x in m]
+            left[h] = left[h] - sum(m[i] * wl[i] for i in range(q))
+            right[h] = right[h] - sum(m[i] * wr[i] for i in range(q))
+    return jnp.concatenate(inverse, axis=0)
+
+
+def orthonormalize(scale, gram_ref, series_ref, basis_ref):
+    gram = gram_ref[...]
+    half = WIDTH
+    row = lax.broadcasted_iota(jnp.int32, gram.shape, 0)
+    column = lax.broadcasted_iota(jnp.int32, gram.shape, 1)
+    diagonal = jnp.where(row == column, gram, 0.0)
+    over_columns = lax.rsqrt(jnp.sum(diagonal, axis=0, keepdims=True))
+    over_rows = lax.rsqrt(jnp.sum(diagonal, axis=1, keepdims=True))
+    gram = gram * over_rows * over_columns
+    series = series_ref[...].T * (over_columns * scale)
+    tiles = range(0, half, 8)
+    first = inverse_factor([gram[i : i + 8, :half] for i in tiles])
+    upper = dot(first, gram[:half, half:], NN)
+    lower = dot(gram[half:, :half], first, NT)
+    rest = gram[half:, half:] - dot(lower, upper, NN)
+    solved = dot(series[:, :half], first, NT)
+    basis_ref[:, :half] = solved
+    left_over = series[:, half:] - dot(solved, upper, NN)
+    second = inverse_factor([rest[i : i + 8, :] for i in tiles])
+    basis_ref[:, half:] = dot(left_over, second, NT)
 
 
 def per_device(sizes, signal, filters):
@@ -237,11 +328,14 @@
         name="project_and_sum",
     )(signal, filters.reshape(sensors * lags, depth))
     sample_count = length * nz * ny
-    lower = jnp.linalg.cholesky(gram)
-    solved = lax.linalg.triangular_solve(
-        lower, series.T, left_side=False, lower=True, transpose_a=True
-    )
-    return solved * math.sqrt(sample_count)
+    return pl.pallas_call(
+        functools.partial(orthonormalize, math.sqrt(sample_count)),
+        out_shape=jax.ShapeDtypeStruct((rows, depth), f32),
+        in_specs=[vmem, vmem],
+        out_specs=vmem,
+        compiler_params=pltpu.CompilerParams(vmem_limit_bytes=48 << 20),
+        name="orthonormalize",
+    )(gram, series)
 
 
 def solution(mesh):

time: 125 us -> 73.1 us (0.58)
  other arithmetic: 54 us -> 0 us
  Pallas kernels: 60.2 us -> 70.8 us
  local copies, waits for them, and re-layouts: 7.29 us -> 2.21 us
  between operations: 1.47 us -> 0.01 us
  matrix products: 1.38 us -> 0 us
    another operation x9 -> x0, other arithmetic: 53.9 us -> none  [the longest x6 34 us: per_device(): lower = jnp.linalg.cholesky(gram)]
    pallas_call x0 -> x1, Pallas kernels: none -> 10.6 us  [per_device(): pl.pallas_call(functools.partial(orthonormalize, math.sqrt(sample_count))...]
    another operation x9 -> x0, local copies, waits for them, and re-layouts: 4.12 us -> none
    another operation x5 -> x0, matrix products: 1.38 us -> none  [the longest x3 0.9 us: per_device(): lax.linalg.triangular_solve(lower, series.T, left_side=False, lower=True,...]
where the time goes in v2:
time: 73.1 us; the launch traced here: 73 us
  Pallas kernels  70.8 us (97%)
  local copies, waits for them, and re-layouts  2.21 us (3%)
    pallas_call x1, Pallas kernels, per_device(): pl.pallas_call(functools.partial(project_and_sum, sizes, lags), out_shape...  60.2 us
    pallas_call x1, Pallas kernels, per_device(): pl.pallas_call(functools.partial(orthonormalize, math.sqrt(sample_count))...  10.6 us
    unnamed x4, local copies, waits for them, and re-layouts  2.21 us

profile of v2, /device:TPU:1, one launch (start us, length us, event | category | flops | bytes accessed | tf_op | source)
XLA Modules:
  0.0 73.0 jit_solution(143008292436271422)
XLA Ops:
  0.0 0.0 copy-start
  0.0 1.3 %copy-done = bf16[38,64,256]{2,1,0:T(8,128)(2,1)S(1)} copy-done((bf16[38,64,256]{2,1,0:T(8,128)(2,1)S(1)}, bf16[38,64,256]{2,1,0:T(8,128)(2,1)}, u32[]{:S(2)}) %copy-start) | copy-done | bytes 1245208
  1.3 0.0 copy-start.1
  1.3 0.9 %copy-done.1 = bf16[38,2048]{1,0:T(8,128)(2,1)S(1)} copy-done((bf16[38,2048]{1,0:T(8,128)(2,1)S(1)}, bf16[38,2048]{1,0:T(8,128)(2,1)}, u32[]{:S(2)}) %copy-start.1) | copy-done | bytes 155672
  2.2 60.2 %project_and_sum.1 = (f32[256,256]{1,0:T(8,128)S(1)}, f32[256,256]{1,0:T(8,128)S(1)}) custom-call(bf16[38,2048]{1,0:T(8,128)(2,1)S(1)} %copy-done.1, bf16[2432,256]{1,0:T(8,128)(2,1)S(1)} %bitcast.1), custom_call_target="tpu_custom_call" | custom-call | tf_op jit(solution)/shard_map/project_and_sum/pallas_call | solution.py:300
  62.4 10.6 %orthonormalize.1 = f32[256,256]{1,0:T(8,128)} custom-call(f32[256,256]{1,0:T(8,128)S(1)} %get-tuple-element.7.gram_ref, f32[256,256]{1,0:T(8,128)S(1)} %get-tuple-element.8.series_ref), custom_call_target="tpu_custom_call" | custom-call | tf_op jit(solution)/shard_map/orthonormalize/pallas_call | solution.py:331
Async XLA Ops:
  0.0 1.3 %copy-start = (bf16[38,64,256]{2,1,0:T(8,128)(2,1)S(1)}, bf16[38,64,256]{2,1,0:T(8,128)(2,1)}, u32[]{:S(2)}) copy-start(bf16[38,64,256]{2,1,0:T(8,128)(2,1)} %param.3) | copy-start | bytes 3735556
  1.3 0.9 %copy-start.1 = (bf16[38,2048]{1,0:T(8,128)(2,1)S(1)}, bf16[38,2048]{1,0:T(8,128)(2,1)}, u32[]{:S(2)}) copy-start(bf16[38,2048]{1,0:T(8,128)(2,1)} %signal.1) | copy-start | bytes 466948

commit v3 on v2

--- a/solution.py
+++ b/solution.py
@@ -15,9 +15,12 @@
 MESH = pl.DeviceIdType.MESH
 HIGHEST = lax.Precision.HIGHEST
 WIDTH = 128
-
-
-def reversed_and_turned(filters, turned, lags):
+TOGETHER = 8
+COUNTS = 31800.0
+BIAS = 125.0
+
+
+def reversed_and_turned(filters, turned, lags, arrivals):
     count = filters.shape[0]
     row = lax.broadcasted_iota(jnp.int32, (256, 256), 0)
     column = lax.broadcasted_iota(jnp.int32, (256, 256), 1)
@@ -25,36 +28,64 @@
     flip = flip.astype(jnp.bfloat16)
     for first in range(0, count, 256):
         n = min(256, count - first)
+        if first in arrivals:
+            arrivals[first].wait()
         block = jnp.dot(
             flip[:n, :n], filters[first : first + n, :], preferred_element_type=jnp.float32
         )
         turned[:, first : first + n] = block.T.astype(jnp.bfloat16)
 
 
-def lagged(wide, hankel, lags, sensors, start, width):
+def projected(wide, turned, hankel, lags, sensors, start, width):
     row = lax.broadcasted_iota(jnp.int32, (lags, WIDTH), 0)
     lane = lax.broadcasted_iota(jnp.int32, (lags, WIDTH), 1)
     first = WIDTH - lags + 1
     inside = lane < first + row
     tiles = width // WIDTH
-    for c in range(sensors):
-        turned = []
-        for j in range(tiles + 1):
-            line = wide[c : c + 1, pl.ds(pl.multiple_of(start + WIDTH * j, WIDTH), WIDTH)]
-            line = jnp.broadcast_to(line, (lags, WIDTH))
-            turned.append(pltpu.roll(line, first, 1, stride=1, stride_axis=0))
-        for j in range(tiles):
-            tile = jnp.where(inside, turned[j], turned[j + 1])
-            hankel[c * lags : (c + 1) * lags, WIDTH * j : WIDTH * (j + 1)] = tile.astype(
-                jnp.bfloat16
-            )
+    total = None
+    for begin in range(0, sensors, TOGETHER):
+        end = min(begin + TOGETHER, sensors)
+        for c in range(begin, end):
+            rolled = []
+            for j in range(tiles + 1):
+                line = wide[c : c + 1, pl.ds(pl.multiple_of(start + WIDTH * j, WIDTH), WIDTH)]
+                line = jnp.broadcast_to(line, (lags, WIDTH))
+                rolled.append(pltpu.roll(line, first, 1, stride=1, stride_axis=0))
+            for j in range(tiles):
+                tile = jnp.where(inside, rolled[j], rolled[j + 1])
+                hankel[c * lags : (c + 1) * lags, WIDTH * j : WIDTH * (j + 1)] = tile.astype(
+                    jnp.bfloat16
+                )
+        depth = slice(begin * lags, end * lags)
+        part = jnp.dot(turned[:, depth], hankel[depth, :], preferred_element_type=jnp.float32)
+        total = part if total is None else total + part
+    return total
+
+
+def coded(block):
+    most = jnp.max(jnp.abs(block), axis=0, keepdims=True)
+    most = jnp.maximum(most * 1.0078125, 1e-30).astype(jnp.bfloat16)
+    count = jnp.floor(jnp.abs(block) * (COUNTS / most.astype(jnp.float32)) + 0.5)
+    high = jnp.floor(count * (1 / 128))
+    value = (1.0 + (count * (1 / 128) - high)) * jnp.exp2(high - BIAS)
+    value = jnp.where(block < 0.0, -value, value).astype(jnp.bfloat16)
+    return value, jnp.broadcast_to(most, (16, block.shape[1]))
+
+
+def decoded(value, most):
+    value = value.astype(jnp.float32)
+    size = jnp.abs(value)
+    exponent = jnp.floor(jnp.log2(size) + 0.003)
+    fraction = jnp.floor(size * jnp.exp2(-exponent) * 128.0 + 0.5)
+    count = exponent * 128.0 + (fraction + (128.0 * BIAS - 128.0))
+    return jnp.where(value < 0.0, -count, count) * (most[:1].astype(jnp.float32) * (1 / COUNTS))
 
 
 def project_and_sum(
-    sizes, lags, signal, filters, series_out, gram_out,
-    wide, turned, hankel, edge, parts, from_core, to_chips, from_chips,
+    sizes, lags, signal_in, filters_in, series_out, gram_out,
+    signal, filters, wide, turned, hankel, edge, parts, from_core, to_chips, from_chips,
     gram, scattered, shard, from_line,
-    edge_send, edge_recv, core_send, core_recv, chip_send, chip_recv,
+    signal_here, filters_here, near, far, edge_send, edge_recv, core_send, core_recv, chip_send, chip_recv,
     scatter_send, scatter_recv, line_send, line_recv, gather_send, gather_recv,
 ):
     nz, ny, nx, nc = sizes
@@ -70,29 +101,45 @@
 
     steps = [(dy, dx, dc) for dy in range(ny) for dx in range(nx) for dc in range(nc)][1:]
     neighbours = [plane(*s) for s in steps]
-    line = [(lax.rem(z + d, nz), y, x, core) for d in range(1, nz)]
+    away = sorted(range(1, nz), key=lambda d: -min(d, nz - d))
+    line = [(lax.rem(z + d, nz), y, x, core) for d in away]
+    along = {d: (lax.rem(z + d + nz, nz), y, x, core) for d in (-4, -2, -1, 1, 2, 4)}
+    column = [plane(d, 0, 0) for d in range(1, ny)]
+    group = [plane(0, dx, dc) for dx in range(nx) for dc in range(nc)][1:]
     behind = (before // ny, lax.rem(before, ny), x, core)
     ahead = (after // ny, lax.rem(after, ny), x, core)
 
+    arrivals = {}
+    signal_copy = pltpu.make_async_copy(signal_in, signal, signal_here)
+    signal_copy.start()
+    every = 512
+    for n, first in enumerate(range(0, filters.shape[0], every)):
+        rows = pl.ds(first, min(every, filters.shape[0] - first))
+        arrivals[first] = pltpu.make_async_copy(
+            filters_in.at[rows], filters.at[rows], filters_here.at[n]
+        )
+        arrivals[first].start()
+
     barrier = pltpu.get_barrier_semaphore()
-    everyone = neighbours + line + [behind, ahead]
-    for device in everyone:
+    first_round = group + column + [along[d] for d in (-2, -1, 1, 2)] + [behind, ahead]
+    for device in first_round:
         pl.semaphore_signal(barrier, inc=1, device_id=device, device_id_type=MESH)
 
+    signal_copy.wait()
     wide[:sensors, :length] = signal[...].astype(jnp.float32)
     edge[0, :sensors, :] = signal[:, :WIDTH]
-    reversed_and_turned(filters, turned, lags)
-    pl.semaphore_wait(barrier, len(everyone))
+    reversed_and_turned(filters, turned, lags, arrivals)
+    pl.semaphore_wait(barrier, len(first_round))
+    second_round = column + [along[-2], along[2]]
+    for device in second_round:
+        pl.semaphore_signal(near, inc=1, device_id=device, device_id_type=MESH)
 
     edge_copy = pltpu.make_async_remote_copy(
         edge.at[0], edge.at[1], edge_send, edge_recv, device_id=behind, device_id_type=MESH
     )
     edge_copy.start()
-    edge_copy.wait()
-    following = edge[1, :sensors, :].astype(jnp.float32)
-    wide[:sensors, length:] = jnp.where(rank == shards - 1, jnp.zeros_like(following), following)
-
-    rows = from_core.shape[2]
+
+    depth, rows = from_core.shape[1:]
     partner = plane(0, 0, 1)
     other = 1 - core
 
@@ -103,23 +150,39 @@
         )
 
     def distance(i):
-        return jnp.where(i == 0, 2, jnp.where(i == 1, 1, jnp.where(i == 2, 3, 0)))
+        first = jnp.where(x == 1, 3, 2)
+        second = jnp.where(x == 2, 3, 1)
+        third = jnp.where(x == 1, 2, jnp.where(x == 2, 1, 3))
+        return jnp.where(i == 0, first, jnp.where(i == 1, second, jnp.where(i == 2, third, 0)))
 
     def to_chip(i):
+        n = distance(i) - 1
         return pltpu.make_async_remote_copy(
-            to_chips.at[i], from_chips.at[i], chip_send.at[i], chip_recv.at[i],
-            device_id=plane(0, distance(i), 0), device_id_type=MESH,
+            to_chips.at[n], from_chips.at[n], chip_send.at[n], chip_recv.at[n],
+            device_id=plane(0, n + 1, 0), device_id_type=MESH,
         )
 
     def pass_on(i):
         to_core(i).wait_recv()
-        to_chips[i] = parts[i, core] + from_core[i]
+        n = distance(i) - 1
+        value, most = coded(parts[i, core] + from_core[i])
+        to_chips[n, :depth, :] = value
+        to_chips[n, depth:, :] = most
         to_chip(i).start()
 
     def step(i, carry):
+        @pl.when(i == 2)
+        def _():
+            edge_copy.wait()
+            following = edge[1, :sensors, :].astype(jnp.float32)
+            following = jnp.where(rank == shards - 1, jnp.zeros_like(following), following)
+            wide[:sensors, length:] = following
+            pl.semaphore_wait(near, len(second_round))
+            for device in (along[-4], along[4]):
+                pl.semaphore_signal(far, inc=1, device_id=device, device_id_type=MESH)
+
         chip = lax.rem(x + distance(i), nx)
-        lagged(wide, hankel, lags, sensors, chip * (2 * rows), 2 * rows)
-        part = jnp.dot(turned[...], hankel[...], preferred_element_type=jnp.float32)
+        part = projected(wide, turned, hankel, lags, sensors, chip * (2 * rows), 2 * rows)
         parts[i, 0] = part[:, :rows]
         parts[i, 1] = part[:, rows:]
         to_core(i).start()
@@ -135,7 +198,8 @@
     own = parts[nx - 1, core] + from_core[nx - 1]
     for i in range(nx - 1):
         to_chip(i).wait_recv()
-        own = own + from_chips[i]
+        n = distance(i) - 1
+        own = own + decoded(from_chips[n, :depth, :], from_chips[n, depth:, :])
     series_out[...] = own
     gram[...] = lax.dot_general(
         own, own, (((1,), (1,)), ((), ())), precision=HIGHEST, preferred_element_type=jnp.float32
@@ -164,6 +228,7 @@
         total = total + scattered[n]
     shard[...] = total
 
+    pl.semaphore_wait(far, 2)
     lines = [
         pltpu.make_async_remote_copy(
             shard, from_line.at[n], line_send.at[n], line_recv.at[n],
@@ -295,6 +360,7 @@
     height = depth // group
     high = -(-sensors // 16) * 16
     vmem = pl.BlockSpec(memory_space=pltpu.VMEM)
+    hbm = pl.BlockSpec(memory_space=pltpu.HBM)
     f32, bf16 = jnp.float32, jnp.bfloat16
     dma = pltpu.SemaphoreType.DMA
     series, gram = pl.pallas_call(
@@ -303,27 +369,30 @@
             jax.ShapeDtypeStruct((depth, rows), f32),
             jax.ShapeDtypeStruct((depth, depth), f32),
         ),
-        in_specs=[vmem, vmem],
+        in_specs=[hbm, hbm],
         out_specs=(vmem, vmem),
         scratch_shapes=[
+            pltpu.VMEM((sensors, length), bf16),
+            pltpu.VMEM((sensors * lags, depth), bf16),
             pltpu.VMEM((high, length + WIDTH), f32),
             pltpu.VMEM((depth, sensors * lags), bf16),
             pltpu.VMEM((sensors * lags, 2 * rows), bf16),
             pltpu.VMEM((2, high, WIDTH), bf16),
             pltpu.VMEM((nx, nc, depth, rows), f32),
             pltpu.VMEM((nx, depth, rows), f32),
-            pltpu.VMEM((nx - 1, depth, rows), f32),
-            pltpu.VMEM((nx - 1, depth, rows), f32),
+            pltpu.VMEM((nx - 1, depth + 16, rows), bf16),
+            pltpu.VMEM((nx - 1, depth + 16, rows), bf16),
             pltpu.VMEM((depth, depth), f32),
             pltpu.VMEM((group - 1, height, depth), f32),
             pltpu.VMEM((height, depth), f32),
             pltpu.VMEM((nz - 1, height, depth), f32),
+            dma, dma((-(-sensors * lags // 512),)), pltpu.SemaphoreType.REGULAR, pltpu.SemaphoreType.REGULAR,
             dma, dma, dma((nx,)), dma((nx,)), dma((nx - 1,)), dma((nx - 1,)),
             dma((group - 1,)), dma((group - 1,)), dma((nz - 1,)), dma((nz - 1,)),
             dma((group - 1,)), dma((group - 1,)),
         ],
         compiler_params=pltpu.CompilerParams(
-            collective_id=0, has_side_effects=True, vmem_limit_bytes=48 << 20
+            collective_id=0, has_side_effects=True, vmem_limit_bytes=40 << 20
         ),
         name="project_and_sum",
     )(signal, filters.reshape(sensors * lags, depth))

time: 73.1 us -> 66.2 us (0.906)
  Pallas kernels: 70.8 us -> 63.8 us
    pallas_call x1, Pallas kernels: 60.2 us -> 53.2 us  [per_device(): pl.pallas_call(functools.partial(project_and_sum, sizes, lags), out_shape...]
where the time goes in v3:
time: 66.2 us; the launch traced here: 66 us
  Pallas kernels  63.8 us (96%)
  local copies, waits for them, and re-layouts  2.21 us (3%)
    pallas_call x1, Pallas kernels, per_device(): pl.pallas_call(functools.partial(project_and_sum, sizes, lags), out_shape...  53.2 us
    pallas_call x1, Pallas kernels, per_device(): pl.pallas_call(functools.partial(orthonormalize, math.sqrt(sample_count))...  10.6 us
    unnamed x4, local copies, waits for them, and re-layouts  2.21 us

profile of v3, /device:TPU:1, one launch (start us, length us, event | category | flops | bytes accessed | tf_op | source)
XLA Modules:
  0.0 66.0 jit_solution(6181968792105326464)
XLA Ops:
  0.0 0.0 copy-start
  0.0 1.3 %copy-done = bf16[38,64,256]{2,1,0:T(8,128)(2,1)S(1)} copy-done((bf16[38,64,256]{2,1,0:T(8,128)(2,1)S(1)}, bf16[38,64,256]{2,1,0:T(8,128)(2,1)}, u32[]{:S(2)}) %copy-start) | copy-done | bytes 1245208
  1.3 0.0 copy-start.1
  1.3 0.9 %copy-done.1 = bf16[38,2048]{1,0:T(8,128)(2,1)S(1)} copy-done((bf16[38,2048]{1,0:T(8,128)(2,1)S(1)}, bf16[38,2048]{1,0:T(8,128)(2,1)}, u32[]{:S(2)}) %copy-start.1) | copy-done | bytes 155672
  2.2 53.2 %project_and_sum.1 = (f32[256,256]{1,0:T(8,128)S(1)}, f32[256,256]{1,0:T(8,128)S(1)}) custom-call(bf16[38,2048]{1,0:T(8,128)(2,1)S(1)} %copy-done.1, bf16[2432,256]{1,0:T(8,128)(2,1)S(1)} %bitcast.1), custom_call_target="tpu_custom_call" | custom-call | tf_op jit(solution)/shard_map/project_and_sum/pallas_call | solution.py:366
  55.5 10.6 %orthonormalize.1 = f32[256,256]{1,0:T(8,128)} custom-call(f32[256,256]{1,0:T(8,128)S(1)} %get-tuple-element.7.gram_ref, f32[256,256]{1,0:T(8,128)S(1)} %get-tuple-element.8.series_ref), custom_call_target="tpu_custom_call" | custom-call | tf_op jit(solution)/shard_map/orthonormalize/pallas_call | solution.py:400
Async XLA Ops:
  0.0 1.3 %copy-start = (bf16[38,64,256]{2,1,0:T(8,128)(2,1)S(1)}, bf16[38,64,256]{2,1,0:T(8,128)(2,1)}, u32[]{:S(2)}) copy-start(bf16[38,64,256]{2,1,0:T(8,128)(2,1)} %param.3) | copy-start | bytes 3735556
  1.3 0.9 %copy-start.1 = (bf16[38,2048]{1,0:T(8,128)(2,1)S(1)}, bf16[38,2048]{1,0:T(8,128)(2,1)}, u32[]{:S(2)}) copy-start(bf16[38,2048]{1,0:T(8,128)(2,1)} %signal_in.1) | copy-start | bytes 466948

commit v4 on v3

v4 whole, which is shorter than its diff:
```python
import functools
import math

import jax
import jax.numpy as jnp
from jax import lax
from jax.experimental import pallas as pl
from jax.experimental.pallas import tpu as pltpu
from jax.sharding import Mesh
from jax.sharding import PartitionSpec as P

AXES = ("z", "y", "x", "core")
CHAN = ("x", "core")
TM = ("z", "y")
MESH = pl.DeviceIdType.MESH
HIGHEST = lax.Precision.HIGHEST
WIDTH = 128
TOGETHER = 8
COUNTS = 31800.0
BIAS = 125.0


def reversed_and_turned(filters, turned, lags, arrivals):
    count = filters.shape[0]
    row = lax.broadcasted_iota(jnp.int32, (256, 256), 0)
    column = lax.broadcasted_iota(jnp.int32, (256, 256), 1)
    flip = jnp.where(row + column == 2 * lags * (row // lags) + lags - 1, 1.0, 0.0)
    flip = flip.astype(jnp.bfloat16)
    for first in range(0, count, 256):
        n = min(256, count - first)
        if first in arrivals:
            arrivals[first].wait()
        block = jnp.dot(
            flip[:n, :n], filters[first : first + n, :], preferred_element_type=jnp.float32
        )
        turned[:, first : first + n] = block.T.astype(jnp.bfloat16)


def projected(wide, turned, hankel, lags, sensors, start, width):
    row = lax.broadcasted_iota(jnp.int32, (lags, WIDTH), 0)
    lane = lax.broadcasted_iota(jnp.int32, (lags, WIDTH), 1)
    first = WIDTH - lags + 1
    inside = lane < first + row
    tiles = width // WIDTH
    total = None
    for begin in range(0, sensors, TOGETHER):
        end = min(begin + TOGETHER, sensors)
        for c in range(begin, end):
            rolled = []
            for j in range(tiles + 1):
                line = wide[c : c + 1, pl.ds(pl.multiple_of(start + WIDTH * j, WIDTH), WIDTH)]
                line = jnp.broadcast_to(line, (lags, WIDTH))
                rolled.append(pltpu.roll(line, first, 1, stride=1, stride_axis=0))
            for j in range(tiles):
                tile = jnp.where(inside, rolled[j], rolled[j + 1])
                hankel[c * lags : (c + 1) * lags, WIDTH * j : WIDTH * (j + 1)] = tile.astype(
                    jnp.bfloat16
                )
        depth = slice(begin * lags, end * lags)
        part = jnp.dot(turned[:, depth], hankel[depth, :], preferred_element_type=jnp.float32)
        total = part if total is None else total + part
    return total


def coded(block):
    most = jnp.max(jnp.abs(block), axis=0, keepdims=True)
    most = jnp.maximum(most * 1.0078125, 1e-30).astype(jnp.bfloat16)
    count = jnp.floor(jnp.abs(block) * (COUNTS / most.astype(jnp.float32)) + 0.5)
    high = jnp.floor(count * (1 / 128))
    value = (1.0 + (count * (1 / 128) - high)) * jnp.exp2(high - BIAS)
    value = jnp.where(block < 0.0, -value, value).astype(jnp.bfloat16)
    return value, jnp.broadcast_to(most, (16, block.shape[1]))


def decoded(value, most):
    value = value.astype(jnp.float32)
    size = jnp.abs(value)
    exponent = jnp.floor(jnp.log2(size) + 0.003)
    fraction = jnp.floor(size * jnp.exp2(-exponent) * 128.0 + 0.5)
    count = exponent * 128.0 + (fraction + (128.0 * BIAS - 128.0))
    return jnp.where(value < 0.0, -count, count) * (most[:1].astype(jnp.float32) * (1 / COUNTS))


NN = ((1,), (0,))
NT = ((1,), (1,))


def dot(a, b, dims):
    return lax.dot_general(
        a, b, (dims, ((), ())), precision=HIGHEST, preferred_element_type=jnp.float32
    )


def spread(x):
    return jnp.broadcast_to(x, (8, WIDTH))


def refined_reciprocal(x):
    r = pltpu.reciprocal(x, approx=True)
    return r * (2.0 - x * r)


def inverse_factor(tiles, q=8):
    count = len(tiles)
    sub = lax.broadcasted_iota(jnp.int32, (8, WIDTH), 0)
    lane = lax.broadcasted_iota(jnp.int32, (8, WIDTH), 1)
    left = list(tiles)
    right = [jnp.where(lane == sub + 8 * g, 1.0, 0.0) for g in range(count)]
    inverse = [jnp.zeros((8, WIDTH), jnp.float32)] * count
    for j in range(0, 8 * count, q):
        g, s = divmod(j, 8)
        rl = [spread(left[g][s + i : s + i + 1, :]) for i in range(q)]
        rr = [spread(right[g][s + i : s + i + 1, :]) for i in range(q)]
        e = {(i, k): spread(rl[i][:, j + k : j + k + 1]) for i in range(q) for k in range(i, q)}
        wl, wr, v = [None] * q, [None] * q, {}
        for i in range(0, q, 2):
            a, b, c = e[i, i], e[i, i + 1], e[i + 1, i + 1]
            inv = refined_reciprocal(a * c - b * b)
            ci, bi, ai = c * inv, b * inv, a * inv
            for k in range(i + 2, q):
                v[i, k] = ci * e[i, k] - bi * e[i + 1, k]
                v[i + 1, k] = ai * e[i + 1, k] - bi * e[i, k]
            for k in range(i + 2, q):
                for m in range(k, q):
                    e[k, m] = e[k, m] - (e[i, k] * v[i, m] + e[i + 1, k] * v[i + 1, m])
            wl[i], wl[i + 1] = ci * rl[i] - bi * rl[i + 1], ai * rl[i + 1] - bi * rl[i]
            wr[i], wr[i + 1] = ci * rr[i] - bi * rr[i + 1], ai * rr[i + 1] - bi * rr[i]
            for k in range(i + 2, q):
                rl[k] = rl[k] - (e[i, k] * wl[i] + e[i + 1, k] * wl[i + 1])
                rr[k] = rr[k] - (e[i, k] * wr[i] + e[i + 1, k] * wr[i + 1])
            root_a = lax.rsqrt(a)
            ratio = b * (root_a * root_a)
            root_c = lax.rsqrt(c - b * ratio)
            first = rr[i] * root_a
            second = (rr[i + 1] - ratio * rr[i]) * root_c
            inverse[g] = jnp.where(
                sub == s + i, first, jnp.where(sub == s + i + 1, second, inverse[g])
            )
        for h in range(g, count):
            if h == g and s + q == 8:
                continue
            m = [spread(left[h][:, j + k : j + k + 1]) for k in range(q)]
            for i in range(0, q, 2):
                for k in range(i + 2, q):
                    m[k] = m[k] - (m[i] * v[i, k] + m[i + 1] * v[i + 1, k])
            if h == g:
                m = [jnp.where(sub >= s + q, x, 0.0) for x in m]
            left[h] = left[h] - sum(m[i] * wl[i] for i in range(q))
            right[h] = right[h] - sum(m[i] * wr[i] for i in range(q))
    return jnp.concatenate(inverse, axis=0)


def orthonormalize(scale, upper_left, upper_right, lower_right, series, basis_ref):
    half = WIDTH
    row = lax.broadcasted_iota(jnp.int32, (half, half), 0)
    column = lax.broadcasted_iota(jnp.int32, (half, half), 1)

    def unit(block):
        diagonal = jnp.where(row == column, block, 0.0)
        return (
            lax.rsqrt(jnp.sum(diagonal, axis=1, keepdims=True)),
            lax.rsqrt(jnp.sum(diagonal, axis=0, keepdims=True)),
        )

    rows_1, columns_1 = unit(upper_left)
    rows_2, columns_2 = unit(lower_right)
    upper_left = upper_left * rows_1 * columns_1
    upper_right = upper_right * rows_1 * columns_2
    lower_right = lower_right * rows_2 * columns_2
    tiles = range(0, half, 8)
    first = inverse_factor([upper_left[i : i + 8] for i in tiles])
    upper = dot(first, upper_right, NN)
    lower = dot(upper_right.T, first, NT)
    rest = lower_right - dot(lower, upper, NN)
    solved = dot(series[:, :half] * (columns_1 * scale), first, NT)
    basis_ref[:, :half] = solved
    left_over = series[:, half:] * (columns_2 * scale) - dot(solved, upper, NN)
    second = inverse_factor([rest[i : i + 8] for i in tiles])
    basis_ref[:, half:] = dot(left_over, second, NT)


def singular_step(
    sizes, lags, signal_in, filters_in, basis_out,
    signal, filters, wide, turned, hankel, edge, parts, from_core, to_chips, from_chips,
    series, packed, scattered, shard, from_line, whole,
    signal_here, filters_here, near, far, edge_send, edge_recv, core_send, core_recv, chip_send, chip_recv,
    scatter_send, scatter_recv, line_send, line_recv, gather_send, gather_recv,
):
    nz, ny, nx, nc = sizes
    z, y, x, core = (lax.axis_index(a) for a in AXES)
    sensors, length = signal.shape
    rank = z * ny + y
    shards = nz * ny
    before = lax.rem(rank + shards - 1, shards)
    after = lax.rem(rank + 1, shards)

    def plane(dy, dx, dc):
        return (z, lax.rem(y + dy, ny), lax.rem(x + dx, nx), lax.rem(core + dc, nc))

    far_first = (2, 1, 3, 0)
    steps = [(dy, dx, dc) for dy in far_first for dx in far_first for dc in range(nc)]
    steps.remove((0, 0, 0))
    neighbours = [plane(*s) for s in steps]
    away = sorted(range(1, nz), key=lambda d: -min(d, nz - d))
    line = [(lax.rem(z + d, nz), y, x, core) for d in away]
    along = {d: (lax.rem(z + d + nz, nz), y, x, core) for d in (-4, -2, -1, 1, 2, 4)}
    column = [plane(d, 0, 0) for d in range(1, ny)]
    group = [plane(0, dx, dc) for dx in range(nx) for dc in range(nc)][1:]
    behind = (before // ny, lax.rem(before, ny), x, core)
    ahead = (after // ny, lax.rem(after, ny), x, core)

    arrivals = {}
    signal_copy = pltpu.make_async_copy(signal_in, signal, signal_here)
    signal_copy.start()
    every = 512
    for n, first in enumerate(range(0, filters.shape[0], every)):
        rows = pl.ds(first, min(every, filters.shape[0] - first))
        arrivals[first] = pltpu.make_async_copy(
            filters_in.at[rows], filters.at[rows], filters_here.at[n]
        )
        arrivals[first].start()

    barrier = pltpu.get_barrier_semaphore()
    first_round = group + column + [along[d] for d in (-2, -1, 1, 2)] + [behind, ahead]
    for device in first_round:
        pl.semaphore_signal(barrier, inc=1, device_id=device, device_id_type=MESH)

    signal_copy.wait()
    wide[:sensors, :length] = signal[...].astype(jnp.float32)
    edge[0, :sensors, :] = signal[:, :WIDTH]
    reversed_and_turned(filters, turned, lags, arrivals)
    pl.semaphore_wait(barrier, len(first_round))
    second_round = column + [along[-2], along[2]]
    for device in second_round:
        pl.semaphore_signal(near, inc=1, device_id=device, device_id_type=MESH)

    edge_copy = pltpu.make_async_remote_copy(
        edge.at[0], edge.at[1], edge_send, edge_recv, device_id=behind, device_id_type=MESH
    )
    edge_copy.start()

    depth, rows = from_core.shape[1:]
    partner = plane(0, 0, 1)
    other = 1 - core

    def to_core(i):
        return pltpu.make_async_remote_copy(
            parts.at[i, other], from_core.at[i], core_send.at[i], core_recv.at[i],
            device_id=partner, device_id_type=MESH,
        )

    def distance(i):
        first = jnp.where(x == 1, 3, 2)
        second = jnp.where(x == 2, 3, 1)
        third = jnp.where(x == 1, 2, jnp.where(x == 2, 1, 3))
        return jnp.where(i == 0, first, jnp.where(i == 1, second, jnp.where(i == 2, third, 0)))

    def to_chip(i):
        n = distance(i) - 1
        return pltpu.make_async_remote_copy(
            to_chips.at[n], from_chips.at[n], chip_send.at[n], chip_recv.at[n],
            device_id=plane(0, n + 1, 0), device_id_type=MESH,
        )

    def pass_on(i):
        to_core(i).wait_recv()
        n = distance(i) - 1
        value, most = coded(parts[i, core] + from_core[i])
        to_chips[n, :depth, :] = value
        to_chips[n, depth:, :] = most
        to_chip(i).start()

    def step(i, carry):
        @pl.when(i == 2)
        def _():
            edge_copy.wait()
            following = edge[1, :sensors, :].astype(jnp.float32)
            following = jnp.where(rank == shards - 1, jnp.zeros_like(following), following)
            wide[:sensors, length:] = following
            pl.semaphore_wait(near, len(second_round))
            for device in (along[-4], along[4]):
                pl.semaphore_signal(far, inc=1, device_id=device, device_id_type=MESH)

        chip = lax.rem(x + distance(i), nx)
        part = projected(wide, turned, hankel, lags, sensors, chip * (2 * rows), 2 * rows)
        parts[i, 0] = part[:, :rows]
        parts[i, 1] = part[:, rows:]
        to_core(i).start()

        @pl.when(i > 0)
        def _():
            pass_on(i - 1)

        return carry

    lax.fori_loop(0, nx, step, 0)
    to_core(nx - 1).wait_recv()
    own = parts[nx - 1, core] + from_core[nx - 1]
    for i in range(nx - 1):
        to_chip(i).wait_recv()
        n = distance(i) - 1
        own = own + decoded(from_chips[n, :depth, :], from_chips[n, depth:, :])
    gram = dot(own, own, NT)
    half = WIDTH
    quarter = 4
    for i in range(half // 8):
        at = slice(8 * i, 8 * i + 8)
        cross = gram[at, half:]
        packed[2 * i, :8] = gram[at, :half]
        packed[2 * i, 8:] = cross[:quarter]
        packed[2 * i + 1, :8] = gram[half + 8 * i : half + 8 * i + 8, half:]
        packed[2 * i + 1, 8:] = cross[quarter:]

    def place(dy, dx, dc):
        _, py, px, pc = plane(dy, dx, dc)
        return (py * nx + px) * nc + pc

    scatters = [
        pltpu.make_async_remote_copy(
            packed.at[place(*s)], scattered.at[n], scatter_send.at[n], scatter_recv.at[n],
            device_id=neighbours[n], device_id_type=MESH,
        )
        for n, s in enumerate(steps)
    ]
    for copy in scatters:
        copy.start()
    series[...] = own.T
    mine = place(0, 0, 0)
    total = packed[mine]
    for n, copy in enumerate(scatters):
        copy.wait_recv()
        total = total + scattered[n]
    shard[...] = total

    pl.semaphore_wait(far, 2)
    lines = [
        pltpu.make_async_remote_copy(
            shard, from_line.at[n], line_send.at[n], line_recv.at[n],
            device_id=device, device_id_type=MESH,
        )
        for n, device in enumerate(line)
    ]
    for copy in lines:
        copy.start()
    for n, copy in enumerate(lines):
        copy.wait_recv()
        total = total + from_line[n]
    whole[mine] = total

    gathers = [
        pltpu.make_async_remote_copy(
            whole.at[mine], whole.at[mine], gather_send.at[n], gather_recv.at[n],
            device_id=neighbours[n], device_id_type=MESH,
        )
        for n in range(len(steps))
    ]
    for copy in gathers:
        copy.start()
    for copy in gathers:
        copy.wait_recv()

    tiles = range(half // 8)
    upper_left = jnp.concatenate([whole[2 * i, :8] for i in tiles], axis=0)
    lower_right = jnp.concatenate([whole[2 * i + 1, :8] for i in tiles], axis=0)
    upper_right = jnp.concatenate([whole[2 * i + k, 8:] for i in tiles for k in range(2)], axis=0)
    scale = math.sqrt(length * shards)
    orthonormalize(scale, upper_left, upper_right, lower_right, series, basis_out)

    edge_done = [to_core(i) for i in range(nx)] + [to_chip(i) for i in range(nx - 1)]
    for copy in edge_done + scatters + lines + gathers:
        copy.wait_send()


def per_device(sizes, signal, filters):
    nz, ny, nx, nc = sizes
    sensors, length = signal.shape
    _, lags, depth = filters.shape
    rows = length // (nx * nc)
    group = ny * nx * nc
    share = 3 * WIDTH // group
    high = -(-sensors // 16) * 16
    vmem = pl.BlockSpec(memory_space=pltpu.VMEM)
    hbm = pl.BlockSpec(memory_space=pl.ANY)
    f32, bf16 = jnp.float32, jnp.bfloat16
    dma = pltpu.SemaphoreType.DMA
    return pl.pallas_call(
        functools.partial(singular_step, sizes, lags),
        out_shape=jax.ShapeDtypeStruct((rows, depth), f32),
        in_specs=[hbm, hbm],
        out_specs=vmem,
        scratch_shapes=[
            pltpu.VMEM((sensors, length), bf16),
            pltpu.VMEM((sensors * lags, depth), bf16),
            pltpu.VMEM((high, length + WIDTH), f32),
            pltpu.VMEM((depth, sensors * lags), bf16),
            pltpu.VMEM((sensors * lags, 2 * rows), bf16),
            pltpu.VMEM((2, high, WIDTH), bf16),
            pltpu.VMEM((nx, nc, depth, rows), f32),
            pltpu.VMEM((nx, depth, rows), f32),
            pltpu.VMEM((nx - 1, depth + 16, rows), bf16),
            pltpu.VMEM((nx - 1, depth + 16, rows), bf16),
            pltpu.VMEM((rows, depth), f32),
            pltpu.VMEM((group, share, WIDTH), f32),
            pltpu.VMEM((group - 1, share, WIDTH), f32),
            pltpu.VMEM((share, WIDTH), f32),
            pltpu.VMEM((nz - 1, share, WIDTH), f32),
            pltpu.VMEM((group, share, WIDTH), f32),
            dma, dma((-(-sensors * lags // 512),)), pltpu.SemaphoreType.REGULAR, pltpu.SemaphoreType.REGULAR,
            dma, dma, dma((nx,)), dma((nx,)), dma((nx - 1,)), dma((nx - 1,)),
            dma((group - 1,)), dma((group - 1,)), dma((nz - 1,)), dma((nz - 1,)),
            dma((group - 1,)), dma((group - 1,)),
        ],
        compiler_params=pltpu.CompilerParams(
            collective_id=0, has_side_effects=True, vmem_limit_bytes=56 << 20
        ),
        name="singular_step",
    )(signal, filters.reshape(sensors * lags, depth))


def solution(mesh):
    sizes = (16, 4, 4, 2)
    torus = Mesh(mesh.devices.reshape(sizes), AXES)
    return jax.shard_map(
        functools.partial(per_device, sizes),
        mesh=torus,
        in_specs=(P(CHAN, TM), P(CHAN, None, None)),
        out_specs=P(TM + CHAN, None),
        check_vma=False,
    )
```

time: 66.2 us -> 61.9 us (0.935)
  Pallas kernels: 63.8 us -> 60.1 us
    pallas_call x2 -> x1, Pallas kernels: 63.8 us -> 60.1 us  [per_device(): pl.pallas_call(functools.partial(singular_step, sizes, lags), out_shape=j...]
    unnamed x4 -> x1, local copies, waits for them, and re-layouts: 2.21 us -> 1.67 us
where the time goes in v4:
time: 61.9 us; the launch traced here: 61.8 us
  Pallas kernels  60.1 us (97%)
  local copies, waits for them, and re-layouts  1.67 us (3%)
    pallas_call x1, Pallas kernels, per_device(): pl.pallas_call(functools.partial(singular_step, sizes, lags), out_shape=j...  60.1 us
    unnamed x1, local copies, waits for them, and re-layouts  1.67 us

profile of v4, /device:TPU:1, one launch (start us, length us, event | category | flops | bytes accessed | tf_op | source)
XLA Modules:
  0.0 61.8 jit_solution(12822936911943010047)
XLA Ops:
  0.0 60.1 %singular_step.1 = f32[256,256]{1,0:T(8,128)} custom-call(bf16[38,2048]{1,0:T(8,128)(2,1)} %signal_in.1, bf16[2432,256]{1,0:T(8,128)(2,1)} %bitcast.1), custom_call_target="tpu_custom_call" | custom-call | tf_op jit(solution)/shard_map/singular_step/pallas_call | solution.py:386
  60.1 1.7 %copy.4 = f32[256,256]{1,0:T(8,128)} copy(f32[256,256]{1,0:T(8,128)} %singular_step.1) | data formatting | bytes 524288

commit v5 on v4

--- a/solution.py
+++ b/solution.py
@@ -16,27 +16,28 @@
 HIGHEST = lax.Precision.HIGHEST
 WIDTH = 128
 TOGETHER = 8
+ENTRY = 24
 COUNTS = 31800.0
 BIAS = 125.0
 
 
-def reversed_and_turned(filters, turned, lags, arrivals):
-    count = filters.shape[0]
+def flipping(lags):
     row = lax.broadcasted_iota(jnp.int32, (256, 256), 0)
     column = lax.broadcasted_iota(jnp.int32, (256, 256), 1)
     flip = jnp.where(row + column == 2 * lags * (row // lags) + lags - 1, 1.0, 0.0)
-    flip = flip.astype(jnp.bfloat16)
-    for first in range(0, count, 256):
-        n = min(256, count - first)
-        if first in arrivals:
-            arrivals[first].wait()
+    return flip.astype(jnp.bfloat16)
+
+
+def reversed_and_turned(flip, filters, turned, begin, end):
+    for first in range(begin, end, 256):
+        n = min(256, end - first)
         block = jnp.dot(
             flip[:n, :n], filters[first : first + n, :], preferred_element_type=jnp.float32
         )
         turned[:, first : first + n] = block.T.astype(jnp.bfloat16)
 
 
-def projected(wide, turned, hankel, lags, sensors, start, width):
+def projected(wide, turned, hankel, lags, sensors, start, width, before=None):
     row = lax.broadcasted_iota(jnp.int32, (lags, WIDTH), 0)
     lane = lax.broadcasted_iota(jnp.int32, (lags, WIDTH), 1)
     first = WIDTH - lags + 1
@@ -45,6 +46,8 @@
     total = None
     for begin in range(0, sensors, TOGETHER):
         end = min(begin + TOGETHER, sensors)
+        if before is not None:
+            before(begin, end)
         for c in range(begin, end):
             rolled = []
             for j in range(tiles + 1):
@@ -95,34 +98,45 @@
     return jnp.broadcast_to(x, (8, WIDTH))
 
 
-def refined_reciprocal(x):
-    r = pltpu.reciprocal(x, approx=True)
-    return r * (2.0 - x * r)
-
-
-def inverse_factor(tiles, q=8):
+def inverse_factor(tiles, held):
+    q = 8
     count = len(tiles)
     sub = lax.broadcasted_iota(jnp.int32, (8, WIDTH), 0)
     lane = lax.broadcasted_iota(jnp.int32, (8, WIDTH), 1)
     left = list(tiles)
     right = [jnp.where(lane == sub + 8 * g, 1.0, 0.0) for g in range(count)]
-    inverse = [jnp.zeros((8, WIDTH), jnp.float32)] * count
-    for j in range(0, 8 * count, q):
-        g, s = divmod(j, 8)
-        rl = [spread(left[g][s + i : s + i + 1, :]) for i in range(q)]
-        rr = [spread(right[g][s + i : s + i + 1, :]) for i in range(q)]
-        e = {(i, k): spread(rl[i][:, j + k : j + k + 1]) for i in range(q) for k in range(i, q)}
+    inverse = []
+    for g in range(count):
+        j, slot = q * g, g % 2
+        held[slot, q] = left[g]
+        held[slot, q + 1] = right[g]
+        for k in range(q):
+            held[slot, k] = spread(left[g][:, j + k : j + k + 1])
+        e = {(i, k): spread(held[slot, k, i : i + 1, :]) for i in range(q) for k in range(i, q)}
+        rl = [spread(held[slot, q, i : i + 1, :]) for i in range(q)]
+        rr = [spread(held[slot, q + 1, i : i + 1, :]) for i in range(q)]
         wl, wr, v = [None] * q, [None] * q, {}
+        done = jnp.zeros((8, WIDTH), jnp.float32)
         for i in range(0, q, 2):
             a, b, c = e[i, i], e[i, i + 1], e[i + 1, i + 1]
-            inv = refined_reciprocal(a * c - b * b)
+            det = a * c - b * b
+            rough = pltpu.reciprocal(det, approx=True)
+            refined = 2.0 - det * rough
+            inv = rough * refined
             ci, bi, ai = c * inv, b * inv, a * inv
             for k in range(i + 2, q):
                 v[i, k] = ci * e[i, k] - bi * e[i + 1, k]
                 v[i + 1, k] = ai * e[i + 1, k] - bi * e[i, k]
+            rest = {}
             for k in range(i + 2, q):
                 for m in range(k, q):
-                    e[k, m] = e[k, m] - (e[i, k] * v[i, m] + e[i + 1, k] * v[i + 1, m])
+                    if m < i + 4:
+                        over = (c * e[i, k] - b * e[i + 1, k]) * e[i, m]
+                        over = over + (a * e[i + 1, k] - b * e[i, k]) * e[i + 1, m]
+                        rest[k, m] = e[k, m] - (over * rough) * refined
+                    else:
+                        rest[k, m] = e[k, m] - (e[i, k] * v[i, m] + e[i + 1, k] * v[i + 1, m])
+            e.update(rest)
             wl[i], wl[i + 1] = ci * rl[i] - bi * rl[i + 1], ai * rl[i + 1] - bi * rl[i]
             wr[i], wr[i + 1] = ci * rr[i] - bi * rr[i + 1], ai * rr[i + 1] - bi * rr[i]
             for k in range(i + 2, q):
@@ -131,26 +145,21 @@
             root_a = lax.rsqrt(a)
             ratio = b * (root_a * root_a)
             root_c = lax.rsqrt(c - b * ratio)
-            first = rr[i] * root_a
-            second = (rr[i + 1] - ratio * rr[i]) * root_c
-            inverse[g] = jnp.where(
-                sub == s + i, first, jnp.where(sub == s + i + 1, second, inverse[g])
-            )
-        for h in range(g, count):
-            if h == g and s + q == 8:
-                continue
+            upper = rr[i] * root_a
+            lower = (rr[i + 1] - ratio * rr[i]) * root_c
+            done = jnp.where(sub == i, upper, jnp.where(sub == i + 1, lower, done))
+        inverse.append(done)
+        for h in range(g + 1, count):
             m = [spread(left[h][:, j + k : j + k + 1]) for k in range(q)]
             for i in range(0, q, 2):
                 for k in range(i + 2, q):
                     m[k] = m[k] - (m[i] * v[i, k] + m[i + 1] * v[i + 1, k])
-            if h == g:
-                m = [jnp.where(sub >= s + q, x, 0.0) for x in m]
             left[h] = left[h] - sum(m[i] * wl[i] for i in range(q))
             right[h] = right[h] - sum(m[i] * wr[i] for i in range(q))
     return jnp.concatenate(inverse, axis=0)
 
 
-def orthonormalize(scale, upper_left, upper_right, lower_right, series, basis_ref):
+def orthonormalize(scale, upper_left, upper_right, lower_right, series, basis_ref, held):
     half = WIDTH
     row = lax.broadcasted_iota(jnp.int32, (half, half), 0)
     column = lax.broadcasted_iota(jnp.int32, (half, half), 1)
@@ -168,21 +177,21 @@
     upper_right = upper_right * rows_1 * columns_2
     lower_right = lower_right * rows_2 * columns_2
     tiles = range(0, half, 8)
-    first = inverse_factor([upper_left[i : i + 8] for i in tiles])
+    first = inverse_factor([upper_left[i : i + 8] for i in tiles], held)
     upper = dot(first, upper_right, NN)
     lower = dot(upper_right.T, first, NT)
     rest = lower_right - dot(lower, upper, NN)
     solved = dot(series[:, :half] * (columns_1 * scale), first, NT)
     basis_ref[:, :half] = solved
     left_over = series[:, half:] * (columns_2 * scale) - dot(solved, upper, NN)
-    second = inverse_factor([rest[i : i + 8] for i in tiles])
+    second = inverse_factor([rest[i : i + 8] for i in tiles], held)
     basis_ref[:, half:] = dot(left_over, second, NT)
 
 
 def singular_step(
     sizes, lags, signal_in, filters_in, basis_out,
     signal, filters, wide, turned, hankel, edge, parts, from_core, to_chips, from_chips,
-    series, packed, scattered, shard, from_line, whole,
+    series, packed, scattered, shard, from_line, whole, held,
     signal_here, filters_here, near, far, edge_send, edge_recv, core_send, core_recv, chip_send, chip_recv,
     scatter_send, scatter_recv, line_send, line_recv, gather_send, gather_recv,
 ):
@@ -212,7 +221,7 @@
     arrivals = {}
     signal_copy = pltpu.make_async_copy(signal_in, signal, signal_here)
     signal_copy.start()
-    every = 512
+    every = TOGETHER * lags
     for n, first in enumerate(range(0, filters.shape[0], every)):
         rows = pl.ds(first, min(every, filters.shape[0] - first))
         arrivals[first] = pltpu.make_async_copy(
@@ -228,16 +237,10 @@
     signal_copy.wait()
     wide[:sensors, :length] = signal[...].astype(jnp.float32)
     edge[0, :sensors, :] = signal[:, :WIDTH]
-    reversed_and_turned(filters, turned, lags, arrivals)
-    pl.semaphore_wait(barrier, len(first_round))
     second_round = column + [along[-2], along[2]]
-    for device in second_round:
-        pl.semaphore_signal(near, inc=1, device_id=device, device_id_type=MESH)
-
     edge_copy = pltpu.make_async_remote_copy(
         edge.at[0], edge.at[1], edge_send, edge_recv, device_id=behind, device_id_type=MESH
     )
-    edge_copy.start()
 
     depth, rows = from_core.shape[1:]
     partner = plane(0, 0, 1)
@@ -269,6 +272,29 @@
         to_chips[n, :depth, :] = value
         to_chips[n, depth:, :] = most
         to_chip(i).start()
+
+    def samples_of(i):
+        return lax.rem(x + distance(i), nx) * (2 * rows)
+
+    def hand_over(i, part):
+        parts[i, 0] = part[:, :rows]
+        parts[i, 1] = part[:, rows:]
+        to_core(i).start()
+
+    flip = flipping(lags)
+
+    def before(begin, end):
+        if begin == ENTRY:
+            pl.semaphore_wait(barrier, len(first_round))
+            for device in second_round:
+                pl.semaphore_signal(near, inc=1, device_id=device, device_id_type=MESH)
+            edge_copy.start()
+        arrivals[begin * lags].wait()
+        reversed_and_turned(flip, filters, turned, begin * lags, end * lags)
+
+    hand_over(
+        0, projected(wide, turned, hankel, lags, sensors, samples_of(0), 2 * rows, before)
+    )
 
     def step(i, carry):
         @pl.when(i == 2)
@@ -281,19 +307,11 @@
             for device in (along[-4], along[4]):
                 pl.semaphore_signal(far, inc=1, device_id=device, device_id_type=MESH)
 
-        chip = lax.rem(x + distance(i), nx)
-        part = projected(wide, turned, hankel, lags, sensors, chip * (2 * rows), 2 * rows)
-        parts[i, 0] = part[:, :rows]
-        parts[i, 1] = part[:, rows:]
-        to_core(i).start()
-
-        @pl.when(i > 0)
-        def _():
-            pass_on(i - 1)
-
+        hand_over(i, projected(wide, turned, hankel, lags, sensors, samples_of(i), 2 * rows))
+        pass_on(i - 1)
         return carry
 
-    lax.fori_loop(0, nx, step, 0)
+    lax.fori_loop(1, nx, step, 0)
     to_core(nx - 1).wait_recv()
     own = parts[nx - 1, core] + from_core[nx - 1]
     for i in range(nx - 1):
@@ -364,7 +382,7 @@
     lower_right = jnp.concatenate([whole[2 * i + 1, :8] for i in tiles], axis=0)
     upper_right = jnp.concatenate([whole[2 * i + k, 8:] for i in tiles for k in range(2)], axis=0)
     scale = math.sqrt(length * shards)
-    orthonormalize(scale, upper_left, upper_right, lower_right, series, basis_out)
+    orthonormalize(scale, upper_left, upper_right, lower_right, series, basis_out, held)
 
     edge_done = [to_core(i) for i in range(nx)] + [to_chip(i) for i in range(nx - 1)]
     for copy in edge_done + scatters + lines + gathers:
@@ -405,7 +423,8 @@
             pltpu.VMEM((share, WIDTH), f32),
             pltpu.VMEM((nz - 1, share, WIDTH), f32),
             pltpu.VMEM((group, share, WIDTH), f32),
-            dma, dma((-(-sensors * lags // 512),)), pltpu.SemaphoreType.REGULAR, pltpu.SemaphoreType.REGULAR,
+            pltpu.VMEM((2, 10, 8, WIDTH), f32),
+            dma, dma((-(-sensors // TOGETHER),)), pltpu.SemaphoreType.REGULAR, pltpu.SemaphoreType.REGULAR,
             dma, dma, dma((nx,)), dma((nx,)), dma((nx - 1,)), dma((nx - 1,)),
             dma((group - 1,)), dma((group - 1,)), dma((nz - 1,)), dma((nz - 1,)),
             dma((group - 1,)), dma((group - 1,)),

time: 61.9 us -> 59.7 us (0.964)
  Pallas kernels: 60.1 us -> 57.8 us
    pallas_call x1, Pallas kernels: 60.1 us -> 57.8 us  [per_device(): pl.pallas_call(functools.partial(singular_step, sizes, lags), out_shape=j...]
where the time goes in v5:
time: 59.7 us; the launch traced here: 59.5 us
  Pallas kernels  57.8 us (97%)
  local copies, waits for them, and re-layouts  1.67 us (3%)
    pallas_call x1, Pallas kernels, per_device(): pl.pallas_call(functools.partial(singular_step, sizes, lags), out_shape=j...  57.8 us
    unnamed x1, local copies, waits for them, and re-layouts  1.67 us

profile of v5, /device:TPU:1, one launch (start us, length us, event | category | flops | bytes accessed | tf_op | source)
XLA Modules:
  0.0 59.5 jit_solution(14524182000600945691)
XLA Ops:
  0.0 57.8 %singular_step.1 = f32[256,256]{1,0:T(8,128)} custom-call(bf16[38,2048]{1,0:T(8,128)(2,1)} %signal_in.1, bf16[2432,256]{1,0:T(8,128)(2,1)} %bitcast.1), custom_call_target="tpu_custom_call" | custom-call | tf_op jit(solution)/shard_map/singular_step/pallas_call | solution.py:404
  57.8 1.7 %copy.4 = f32[256,256]{1,0:T(8,128)} copy(f32[256,256]{1,0:T(8,128)} %singular_step.1) | data formatting | bytes 524288

commit v6 on v5

--- a/solution.py
+++ b/solution.py
@@ -159,7 +159,7 @@
     return jnp.concatenate(inverse, axis=0)
 
 
-def orthonormalize(scale, upper_left, upper_right, lower_right, series, basis_ref, held):
+def orthonormalize(scale, gathered, series, basis_ref, held):
     half = WIDTH
     row = lax.broadcasted_iota(jnp.int32, (half, half), 0)
     column = lax.broadcasted_iota(jnp.int32, (half, half), 1)
@@ -171,18 +171,20 @@
             lax.rsqrt(jnp.sum(diagonal, axis=0, keepdims=True)),
         )
 
+    tiles = range(0, half, 8)
+    upper_left = gathered(0)
     rows_1, columns_1 = unit(upper_left)
+    upper_left = upper_left * rows_1 * columns_1
+    first = inverse_factor([upper_left[i : i + 8] for i in tiles], held)
+    solved = dot(series[:, :half] * (columns_1 * scale), first, NT)
+    basis_ref[:, :half] = solved
+    upper_right, lower_right = gathered(1)
     rows_2, columns_2 = unit(lower_right)
-    upper_left = upper_left * rows_1 * columns_1
     upper_right = upper_right * rows_1 * columns_2
     lower_right = lower_right * rows_2 * columns_2
-    tiles = range(0, half, 8)
-    first = inverse_factor([upper_left[i : i + 8] for i in tiles], held)
     upper = dot(first, upper_right, NN)
     lower = dot(upper_right.T, first, NT)
     rest = lower_right - dot(lower, upper, NN)
-    solved = dot(series[:, :half] * (columns_1 * scale), first, NT)
-    basis_ref[:, :half] = solved
     left_over = series[:, half:] * (columns_2 * scale) - dot(solved, upper, NN)
     second = inverse_factor([rest[i : i + 8] for i in tiles], held)
     basis_ref[:, half:] = dot(left_over, second, NT)
@@ -191,7 +193,8 @@
 def singular_step(
     sizes, lags, signal_in, filters_in, basis_out,
     signal, filters, wide, turned, hankel, edge, parts, from_core, to_chips, from_chips,
-    series, packed, scattered, shard, from_line, whole, held,
+    series, packed_a, scattered_a, shard_a, from_line_a, whole_a,
+    packed_b, scattered_b, shard_b, from_line_b, whole_b, held,
     signal_here, filters_here, near, far, edge_send, edge_recv, core_send, core_recv, chip_send, chip_recv,
     scatter_send, scatter_recv, line_send, line_recv, gather_send, gather_recv,
 ):
@@ -318,74 +321,99 @@
         to_chip(i).wait_recv()
         n = distance(i) - 1
         own = own + decoded(from_chips[n, :depth, :], from_chips[n, depth:, :])
-    gram = dot(own, own, NT)
     half = WIDTH
-    quarter = 4
-    for i in range(half // 8):
-        at = slice(8 * i, 8 * i + 8)
-        cross = gram[at, half:]
-        packed[2 * i, :8] = gram[at, :half]
-        packed[2 * i, 8:] = cross[:quarter]
-        packed[2 * i + 1, :8] = gram[half + 8 * i : half + 8 * i + 8, half:]
-        packed[2 * i + 1, 8:] = cross[quarter:]
+    groups = [(packed_a, scattered_a, shard_a, from_line_a, whole_a)]
+    groups.append((packed_b, scattered_b, shard_b, from_line_b, whole_b))
 
     def place(dy, dx, dc):
         _, py, px, pc = plane(dy, dx, dc)
         return (py * nx + px) * nc + pc
 
-    scatters = [
-        pltpu.make_async_remote_copy(
-            packed.at[place(*s)], scattered.at[n], scatter_send.at[n], scatter_recv.at[n],
-            device_id=neighbours[n], device_id_type=MESH,
-        )
-        for n, s in enumerate(steps)
-    ]
-    for copy in scatters:
-        copy.start()
+    mine = place(0, 0, 0)
+
+    def scatters(g):
+        packed, scattered = groups[g][:2]
+        return [
+            pltpu.make_async_remote_copy(
+                packed.at[place(*s)], scattered.at[n], scatter_send.at[g, n], scatter_recv.at[g, n],
+                device_id=neighbours[n], device_id_type=MESH,
+            )
+            for n, s in enumerate(steps)
+        ]
+
+    def lines(g):
+        shard, from_line = groups[g][2:4]
+        return [
+            pltpu.make_async_remote_copy(
+                shard, from_line.at[n], line_send.at[g, n], line_recv.at[g, n],
+                device_id=device, device_id_type=MESH,
+            )
+            for n, device in enumerate(line)
+        ]
+
+    def gathers(g):
+        whole = groups[g][4]
+        return [
+            pltpu.make_async_remote_copy(
+                whole.at[mine], whole.at[mine], gather_send.at[g, n], gather_recv.at[g, n],
+                device_id=neighbours[n], device_id_type=MESH,
+            )
+            for n in range(len(steps))
+        ]
+
+    def start(copies):
+        for copy in copies:
+            copy.start()
+
+    tiles = range(half // 8)
+    upper_left = dot(own[:half], own[:half], NT)
+    for i in tiles:
+        packed_a[2 * i] = upper_left[8 * i : 8 * i + 4]
+        packed_a[2 * i + 1] = upper_left[8 * i + 4 : 8 * i + 8]
+    start(scatters(0))
+    upper_right = dot(own[:half], own[half:], NT)
+    lower_right = dot(own[half:], own[half:], NT)
+    for i in tiles:
+        packed_b[2 * i] = upper_right[8 * i : 8 * i + 8]
+        packed_b[2 * i + 1] = lower_right[8 * i : 8 * i + 8]
+    start(scatters(1))
     series[...] = own.T
-    mine = place(0, 0, 0)
-    total = packed[mine]
-    for n, copy in enumerate(scatters):
-        copy.wait_recv()
-        total = total + scattered[n]
-    shard[...] = total
-
-    pl.semaphore_wait(far, 2)
-    lines = [
-        pltpu.make_async_remote_copy(
-            shard, from_line.at[n], line_send.at[n], line_recv.at[n],
-            device_id=device, device_id_type=MESH,
-        )
-        for n, device in enumerate(line)
-    ]
-    for copy in lines:
-        copy.start()
-    for n, copy in enumerate(lines):
-        copy.wait_recv()
-        total = total + from_line[n]
-    whole[mine] = total
-
-    gathers = [
-        pltpu.make_async_remote_copy(
-            whole.at[mine], whole.at[mine], gather_send.at[n], gather_recv.at[n],
-            device_id=neighbours[n], device_id_type=MESH,
-        )
-        for n in range(len(steps))
-    ]
-    for copy in gathers:
-        copy.start()
-    for copy in gathers:
-        copy.wait_recv()
-
-    tiles = range(half // 8)
-    upper_left = jnp.concatenate([whole[2 * i, :8] for i in tiles], axis=0)
-    lower_right = jnp.concatenate([whole[2 * i + 1, :8] for i in tiles], axis=0)
-    upper_right = jnp.concatenate([whole[2 * i + k, 8:] for i in tiles for k in range(2)], axis=0)
+    totals = []
+    for g in range(2):
+        total = groups[g][0][mine]
+        for n, copy in enumerate(scatters(g)):
+            copy.wait_recv()
+            total = total + groups[g][1][n]
+        groups[g][2][...] = total
+        if g == 0:
+            pl.semaphore_wait(far, 2)
+        start(lines(g))
+        totals.append(total)
+    for g in range(2):
+        total = totals[g]
+        for n, copy in enumerate(lines(g)):
+            copy.wait_recv()
+            total = total + groups[g][3][n]
+        groups[g][4][mine] = total
+        start(gathers(g))
+
+    def gathered(g):
+        for copy in gathers(g):
+            copy.wait_recv()
+        whole = groups[g][4]
+        if g == 0:
+            return jnp.concatenate([whole[i] for i in range(2 * half // 8)], axis=0)
+        return tuple(
+            jnp.concatenate([whole[2 * i + k] for i in tiles], axis=0) for k in range(2)
+        )
+
     scale = math.sqrt(length * shards)
-    orthonormalize(scale, upper_left, upper_right, lower_right, series, basis_out, held)
-
-    edge_done = [to_core(i) for i in range(nx)] + [to_chip(i) for i in range(nx - 1)]
-    for copy in edge_done + scatters + lines + gathers:
+    orthonormalize(scale, gathered, series, basis_out, held)
+
+    sent = [to_core(i) for i in range(nx)] + [to_chip(i) for i in range(nx - 1)]
+    for g in range(2):
+        sent += scatters(g) + lines(g) + gathers(g)
+    for copy in sent:
         copy.wait_send()
 
 
@@ -395,7 +423,7 @@
     _, lags, depth = filters.shape
     rows = length // (nx * nc)
     group = ny * nx * nc
-    share = 3 * WIDTH // group
+    few, many = WIDTH // group, 2 * WIDTH // group
     high = -(-sensors // 16) * 16
     vmem = pl.BlockSpec(memory_space=pltpu.VMEM)
     hbm = pl.BlockSpec(memory_space=pl.ANY)
@@ -418,16 +446,21 @@
             pltpu.VMEM((nx - 1, depth + 16, rows), bf16),
             pltpu.VMEM((nx - 1, depth + 16, rows), bf16),
             pltpu.VMEM((rows, depth), f32),
-            pltpu.VMEM((group, share, WIDTH), f32),
-            pltpu.VMEM((group - 1, share, WIDTH), f32),
-            pltpu.VMEM((share, WIDTH), f32),
-            pltpu.VMEM((nz - 1, share, WIDTH), f32),
-            pltpu.VMEM((group, share, WIDTH), f32),
+            pltpu.VMEM((group, few, WIDTH), f32),
+            pltpu.VMEM((group - 1, few, WIDTH), f32),
+            pltpu.VMEM((few, WIDTH), f32),
+            pltpu.VMEM((nz - 1, few, WIDTH), f32),
+            pltpu.VMEM((group, few, WIDTH), f32),
+            pltpu.VMEM((group, many, WIDTH), f32),
+            pltpu.VMEM((group - 1, many, WIDTH), f32),
+            pltpu.VMEM((many, WIDTH), f32),
+            pltpu.VMEM((nz - 1, many, WIDTH), f32),
+            pltpu.VMEM((group, many, WIDTH), f32),
             pltpu.VMEM((2, 10, 8, WIDTH), f32),
             dma, dma((-(-sensors // TOGETHER),)), pltpu.SemaphoreType.REGULAR, pltpu.SemaphoreType.REGULAR,
             dma, dma, dma((nx,)), dma((nx,)), dma((nx - 1,)), dma((nx - 1,)),
-            dma((group - 1,)), dma((group - 1,)), dma((nz - 1,)), dma((nz - 1,)),
-            dma((group - 1,)), dma((group - 1,)),
+            dma((2, group - 1)), dma((2, group - 1)), dma((2, nz - 1)), dma((2, nz - 1)),
+            dma((2, group - 1)), dma((2, group - 1)),
         ],
         compiler_params=pltpu.CompilerParams(
             collective_id=0, has_side_effects=True, vmem_limit_bytes=56 << 20

time: 59.7 us -> 59.9 us (level)
  no operation moved by 1% of the time
where the time goes in v6:
time: 59.9 us; the launch traced here: 59.8 us
  Pallas kernels  58.1 us (97%)
  local copies, waits for them, and re-layouts  1.67 us (3%)
    pallas_call x1, Pallas kernels, per_device(): pl.pallas_call(functools.partial(singular_step, sizes, lags), out_shape=j...  58.1 us
    unnamed x1, local copies, waits for them, and re-layouts  1.67 us

profile of v6, /device:TPU:1, one launch (start us, length us, event | category | flops | bytes accessed | tf_op | source)
XLA Modules:
  0.0 59.8 jit_solution(7004577315501906022)
XLA Ops:
  0.0 58.1 %singular_step.1 = f32[256,256]{1,0:T(8,128)} custom-call(bf16[38,2048]{1,0:T(8,128)(2,1)} %signal_in.1, bf16[2432,256]{1,0:T(8,128)(2,1)} %bitcast.1), custom_call_target="tpu_custom_call" | custom-call | tf_op jit(solution)/shard_map/singular_step/pallas_call | solution.py:432
  58.1 1.7 %copy.4 = f32[256,256]{1,0:T(8,128)} copy(f32[256,256]{1,0:T(8,128)} %singular_step.1) | data formatting | bytes 524288

commit v7 on v5

--- a/solution.py
+++ b/solution.py
@@ -189,10 +189,10 @@
 
 
 def singular_step(
-    sizes, lags, signal_in, filters_in, basis_out,
-    signal, filters, wide, turned, hankel, edge, parts, from_core, to_chips, from_chips,
+    sizes, lags, signal, filters_in, basis_out,
+    filters, wide, turned, hankel, edge, parts, from_core, to_chips, from_chips,
     series, packed, scattered, shard, from_line, whole, held,
-    signal_here, filters_here, near, far, edge_send, edge_recv, core_send, core_recv, chip_send, chip_recv,
+    filters_here, near, far, edge_send, edge_recv, core_send, core_recv, chip_send, chip_recv,
     scatter_send, scatter_recv, line_send, line_recv, gather_send, gather_recv,
 ):
     nz, ny, nx, nc = sizes
@@ -219,8 +219,6 @@
     ahead = (after // ny, lax.rem(after, ny), x, core)
 
     arrivals = {}
-    signal_copy = pltpu.make_async_copy(signal_in, signal, signal_here)
-    signal_copy.start()
     every = TOGETHER * lags
     for n, first in enumerate(range(0, filters.shape[0], every)):
         rows = pl.ds(first, min(every, filters.shape[0] - first))
@@ -234,7 +232,6 @@
     for device in first_round:
         pl.semaphore_signal(barrier, inc=1, device_id=device, device_id_type=MESH)
 
-    signal_copy.wait()
     wide[:sensors, :length] = signal[...].astype(jnp.float32)
     edge[0, :sensors, :] = signal[:, :WIDTH]
     second_round = column + [along[-2], along[2]]
@@ -404,10 +401,9 @@
     return pl.pallas_call(
         functools.partial(singular_step, sizes, lags),
         out_shape=jax.ShapeDtypeStruct((rows, depth), f32),
-        in_specs=[hbm, hbm],
+        in_specs=[vmem, hbm],
         out_specs=vmem,
         scratch_shapes=[
-            pltpu.VMEM((sensors, length), bf16),
             pltpu.VMEM((sensors * lags, depth), bf16),
             pltpu.VMEM((high, length + WIDTH), f32),
             pltpu.VMEM((depth, sensors * lags), bf16),
@@ -424,13 +420,13 @@
             pltpu.VMEM((nz - 1, share, WIDTH), f32),
             pltpu.VMEM((group, share, WIDTH), f32),
             pltpu.VMEM((2, 10, 8, WIDTH), f32),
-            dma, dma((-(-sensors // TOGETHER),)), pltpu.SemaphoreType.REGULAR, pltpu.SemaphoreType.REGULAR,
+            dma((-(-sensors // TOGETHER),)), pltpu.SemaphoreType.REGULAR, pltpu.SemaphoreType.REGULAR,
             dma, dma, dma((nx,)), dma((nx,)), dma((nx - 1,)), dma((nx - 1,)),
             dma((group - 1,)), dma((group - 1,)), dma((nz - 1,)), dma((nz - 1,)),
             dma((group - 1,)), dma((group - 1,)),
         ],
         compiler_params=pltpu.CompilerParams(
-            collective_id=0, has_side_effects=True, vmem_limit_bytes=56 << 20
+            collective_id=0, has_side_effects=True, vmem_limit_bytes=54528 << 10
         ),
         name="singular_step",
     )(signal, filters.reshape(sensors * lags, depth))

time: 59.7 us -> 59.1 us (0.990)
    unnamed x1 -> x3, local copies, waits for them, and re-layouts: 1.67 us -> 1.62 us
where the time goes in v7:
time: 59.1 us; the launch traced here: 58.9 us
  Pallas kernels  57.3 us (97%)
  local copies, waits for them, and re-layouts  1.62 us (3%)
    pallas_call x1, Pallas kernels, per_device(): pl.pallas_call(functools.partial(singular_step, sizes, lags), out_shape=j...  57.3 us
    unnamed x3, local copies, waits for them, and re-layouts  1.62 us

profile of v7, /device:TPU:1, one launch (start us, length us, event | category | flops | bytes accessed | tf_op | source)
XLA Modules:
  0.0 58.9 jit_solution(9252591945250365505)
XLA Ops:
  0.0 0.0 copy-start
  0.0 0.9 %copy-done = bf16[38,2048]{1,0:T(8,128)(2,1)S(1)} copy-done((bf16[38,2048]{1,0:T(8,128)(2,1)S(1)}, bf16[38,2048]{1,0:T(8,128)(2,1)}, u32[]{:S(2)}) %copy-start) | copy-done | bytes 155672
  0.9 57.3 %singular_step.1 = f32[256,256]{1,0:T(8,128)S(1)} custom-call(bf16[38,2048]{1,0:T(8,128)(2,1)S(1)} %copy-done, bf16[2432,256]{1,0:T(8,128)(2,1)} %bitcast.1), custom_call_target="tpu_custom_call" | custom-call | tf_op jit(solution)/shard_map/singular_step/pallas_call | solution.py:401
  58.2 0.7 %copy.4 = f32[256,256]{1,0:T(8,128)} copy(f32[256,256]{1,0:T(8,128)S(1)} %singular_step.1) | data formatting | bytes 524288
Async XLA Ops:
  0.0 0.9 %copy-start = (bf16[38,2048]{1,0:T(8,128)(2,1)S(1)}, bf16[38,2048]{1,0:T(8,128)(2,1)}, u32[]{:S(2)}) copy-start(bf16[38,2048]{1,0:T(8,128)(2,1)} %signal.1) | copy-start | bytes 466948

commit v8 on v7

--- a/solution.py
+++ b/solution.py
@@ -149,8 +149,17 @@
             lower = (rr[i + 1] - ratio * rr[i]) * root_c
             done = jnp.where(sub == i, upper, jnp.where(sub == i + 1, lower, done))
         inverse.append(done)
+        fl, fr = list(wl), list(wr)
+        for i in range(q - 3, -1, -1):
+            for k in range(i // 2 * 2 + 2, q):
+                fl[i] = fl[i] - v[i, k] * fl[k]
+                fr[i] = fr[i] - v[i, k] * fr[k]
         for h in range(g + 1, count):
             m = [spread(left[h][:, j + k : j + k + 1]) for k in range(q)]
+            if h > g + 1:
+                left[h] = left[h] - sum(m[i] * fl[i] for i in range(q))
+                right[h] = right[h] - sum(m[i] * fr[i] for i in range(q))
+                continue
             for i in range(0, q, 2):
                 for k in range(i + 2, q):
                     m[k] = m[k] - (m[i] * v[i, k] + m[i + 1] * v[i + 1, k])
@@ -251,8 +260,8 @@
 
     def distance(i):
         first = jnp.where(x == 1, 3, 2)
-        second = jnp.where(x == 2, 3, 1)
-        third = jnp.where(x == 1, 2, jnp.where(x == 2, 1, 3))
+        second = jnp.where(x == 1, 2, jnp.where(x == 2, 3, 1))
+        third = jnp.where(x == 1, 1, jnp.where(x == 2, 1, 3))
         return jnp.where(i == 0, first, jnp.where(i == 1, second, jnp.where(i == 2, third, 0)))
 
     def to_chip(i):
@@ -294,7 +303,7 @@
     )
 
     def step(i, carry):
-        @pl.when(i == 2)
+        @pl.when(i == jnp.where(x == 1, 1, 2))
         def _():
             edge_copy.wait()
             following = edge[1, :sensors, :].astype(jnp.float32)

time: 59.1 us -> 58.8 us (level)
  no operation moved by 1% of the time
where the time goes in v8:
time: 58.8 us; the launch traced here: 58.6 us
  Pallas kernels  57 us (97%)
  local copies, waits for them, and re-layouts  1.62 us (3%)
    pallas_call x1, Pallas kernels, per_device(): pl.pallas_call(functools.partial(singular_step, sizes, lags), out_shape=j...  57 us
    unnamed x3, local copies, waits for them, and re-layouts  1.62 us

profile of v8, /device:TPU:1, one launch (start us, length us, event | category | flops | bytes accessed | tf_op | source)
XLA Modules:
  0.0 58.6 jit_solution(10379370701238984565)
XLA Ops:
  0.0 0.0 copy-start
  0.0 0.9 %copy-done = bf16[38,2048]{1,0:T(8,128)(2,1)S(1)} copy-done((bf16[38,2048]{1,0:T(8,128)(2,1)S(1)}, bf16[38,2048]{1,0:T(8,128)(2,1)}, u32[]{:S(2)}) %copy-start) | copy-done | bytes 155672
  0.9 57.0 %singular_step.1 = f32[256,256]{1,0:T(8,128)S(1)} custom-call(bf16[38,2048]{1,0:T(8,128)(2,1)S(1)} %copy-done, bf16[2432,256]{1,0:T(8,128)(2,1)} %bitcast.1), custom_call_target="tpu_custom_call" | custom-call | tf_op jit(solution)/shard_map/singular_step/pallas_call | solution.py:410
  57.9 0.7 %copy.4 = f32[256,256]{1,0:T(8,128)} copy(f32[256,256]{1,0:T(8,128)S(1)} %singular_step.1) | data formatting | bytes 524288
Async XLA Ops:
  0.0 0.9 %copy-start = (bf16[38,2048]{1,0:T(8,128)(2,1)S(1)}, bf16[38,2048]{1,0:T(8,128)(2,1)}, u32[]{:S(2)}) copy-start(bf16[38,2048]{1,0:T(8,128)(2,1)} %signal.1) | copy-start | bytes 466948

commit v9 on v8

--- a/solution.py
+++ b/solution.py
@@ -366,6 +366,8 @@
     ]
     for copy in lines:
         copy.start()
+    for copy in [to_core(i) for i in range(nx)] + [to_chip(i) for i in range(nx - 1)] + scatters:
+        copy.wait_send()
     for n, copy in enumerate(lines):
         copy.wait_recv()
         total = total + from_line[n]
@@ -380,6 +382,8 @@
     ]
     for copy in gathers:
         copy.start()
+    for copy in lines + gathers:
+        copy.wait_send()
     for copy in gathers:
         copy.wait_recv()
 
@@ -389,10 +393,6 @@
     upper_right = jnp.concatenate([whole[2 * i + k, 8:] for i in tiles for k in range(2)], axis=0)
     scale = math.sqrt(length * shards)
     orthonormalize(scale, upper_left, upper_right, lower_right, series, basis_out, held)
-
-    edge_done = [to_core(i) for i in range(nx)] + [to_chip(i) for i in range(nx - 1)]
-    for copy in edge_done + scatters + lines + gathers:
-        copy.wait_send()
 
 
 def per_device(sizes, signal, filters):

time: 58.8 us -> 58.7 us (level)
  no operation moved by 1% of the time
where the time goes in v9:
time: 58.7 us; the launch traced here: 58.5 us
  Pallas kernels  56.9 us (97%)
  local copies, waits for them, and re-layouts  1.62 us (3%)
    pallas_call x1, Pallas kernels, per_device(): pl.pallas_call(functools.partial(singular_step, sizes, lags), out_shape=j...  56.9 us
    unnamed x3, local copies, waits for them, and re-layouts  1.62 us

profile of v9, /device:TPU:1, one launch (start us, length us, event | category | flops | bytes accessed | tf_op | source)
XLA Modules:
  0.0 58.5 jit_solution(1307594821446765273)
XLA Ops:
  0.0 0.0 copy-start
  0.0 0.9 %copy-done = bf16[38,2048]{1,0:T(8,128)(2,1)S(1)} copy-done((bf16[38,2048]{1,0:T(8,128)(2,1)S(1)}, bf16[38,2048]{1,0:T(8,128)(2,1)}, u32[]{:S(2)}) %copy-start) | copy-done | bytes 155672
  0.9 56.9 %singular_step.1 = f32[256,256]{1,0:T(8,128)S(1)} custom-call(bf16[38,2048]{1,0:T(8,128)(2,1)S(1)} %copy-done, bf16[2432,256]{1,0:T(8,128)(2,1)} %bitcast.1), custom_call_target="tpu_custom_call" | custom-call | tf_op jit(solution)/shard_map/singular_step/pallas_call | solution.py:410
  57.8 0.7 %copy.4 = f32[256,256]{1,0:T(8,128)} copy(f32[256,256]{1,0:T(8,128)S(1)} %singular_step.1) | data formatting | bytes 524288
Async XLA Ops:
  0.0 0.9 %copy-start = (bf16[38,2048]{1,0:T(8,128)(2,1)S(1)}, bf16[38,2048]{1,0:T(8,128)(2,1)}, u32[]{:S(2)}) copy-start(bf16[38,2048]{1,0:T(8,128)(2,1)} %signal.1) | copy-start | bytes 466948

commit v10 on v9

--- a/solution.py
+++ b/solution.py
@@ -17,6 +17,7 @@
 WIDTH = 128
 TOGETHER = 8
 ENTRY = 24
+PASSING = 32
 COUNTS = 31800.0
 BIAS = 125.0
 
@@ -313,8 +314,13 @@
             for device in (along[-4], along[4]):
                 pl.semaphore_signal(far, inc=1, device_id=device, device_id_type=MESH)
 
-        hand_over(i, projected(wide, turned, hankel, lags, sensors, samples_of(i), 2 * rows))
-        pass_on(i - 1)
+        def between(begin, end):
+            if begin == PASSING:
+                pass_on(i - 1)
+
+        hand_over(
+            i, projected(wide, turned, hankel, lags, sensors, samples_of(i), 2 * rows, between)
+        )
         return carry
 
     lax.fori_loop(1, nx, step, 0)

time: 58.7 us -> 59.2 us (level)
  no operation moved by 1% of the time
where the time goes in v10:
time: 59.2 us; the launch traced here: 59 us
  Pallas kernels  57.4 us (97%)
  local copies, waits for them, and re-layouts  1.62 us (3%)
    pallas_call x1, Pallas kernels, per_device(): pl.pallas_call(functools.partial(singular_step, sizes, lags), out_shape=j...  57.4 us
    unnamed x3, local copies, waits for them, and re-layouts  1.62 us

profile of v10, /device:TPU:1, one launch (start us, length us, event | category | flops | bytes accessed | tf_op | source)
XLA Modules:
  0.0 59.0 jit_solution(436426288823841382)
XLA Ops:
  0.0 0.0 copy-start
  0.0 0.9 %copy-done = bf16[38,2048]{1,0:T(8,128)(2,1)S(1)} copy-done((bf16[38,2048]{1,0:T(8,128)(2,1)S(1)}, bf16[38,2048]{1,0:T(8,128)(2,1)}, u32[]{:S(2)}) %copy-start) | copy-done | bytes 155672
  0.9 57.4 %singular_step.1 = f32[256,256]{1,0:T(8,128)S(1)} custom-call(bf16[38,2048]{1,0:T(8,128)(2,1)S(1)} %copy-done, bf16[2432,256]{1,0:T(8,128)(2,1)} %bitcast.1), custom_call_target="tpu_custom_call" | custom-call | tf_op jit(solution)/shard_map/singular_step/pallas_call | solution.py:416
  58.3 0.7 %copy.4 = f32[256,256]{1,0:T(8,128)} copy(f32[256,256]{1,0:T(8,128)S(1)} %singular_step.1) | data formatting | bytes 524288
Async XLA Ops:
  0.0 0.9 %copy-start = (bf16[38,2048]{1,0:T(8,128)(2,1)S(1)}, bf16[38,2048]{1,0:T(8,128)(2,1)}, u32[]{:S(2)}) copy-start(bf16[38,2048]{1,0:T(8,128)(2,1)} %signal.1) | copy-start | bytes 466948

commit v11 on v9

--- a/solution.py
+++ b/solution.py
@@ -16,7 +16,7 @@
 HIGHEST = lax.Precision.HIGHEST
 WIDTH = 128
 TOGETHER = 8
-ENTRY = 24
+ENTRY = 16
 COUNTS = 31800.0
 BIAS = 125.0
 

time: 58.7 us -> 58.7 us (level)
  no operation moved by 1% of the time
where the time goes in v11:
time: 58.7 us; the launch traced here: 58.6 us
  Pallas kernels  57 us (97%)
  local copies, waits for them, and re-layouts  1.62 us (3%)
    pallas_call x1, Pallas kernels, per_device(): pl.pallas_call(functools.partial(singular_step, sizes, lags), out_shape=j...  57 us
    unnamed x3, local copies, waits for them, and re-layouts  1.62 us

profile of v11, /device:TPU:1, one launch (start us, length us, event | category | flops | bytes accessed | tf_op | source)
XLA Modules:
  0.0 58.6 jit_solution(2645874346499839180)
XLA Ops:
  0.0 0.0 copy-start
  0.0 0.9 %copy-done = bf16[38,2048]{1,0:T(8,128)(2,1)S(1)} copy-done((bf16[38,2048]{1,0:T(8,128)(2,1)S(1)}, bf16[38,2048]{1,0:T(8,128)(2,1)}, u32[]{:S(2)}) %copy-start) | copy-done | bytes 155672
  0.9 57.0 %singular_step.1 = f32[256,256]{1,0:T(8,128)S(1)} custom-call(bf16[38,2048]{1,0:T(8,128)(2,1)S(1)} %copy-done, bf16[2432,256]{1,0:T(8,128)(2,1)} %bitcast.1), custom_call_target="tpu_custom_call" | custom-call | tf_op jit(solution)/shard_map/singular_step/pallas_call | solution.py:410
  57.9 0.7 %copy.4 = f32[256,256]{1,0:T(8,128)} copy(f32[256,256]{1,0:T(8,128)S(1)} %singular_step.1) | data formatting | bytes 524288
Async XLA Ops:
  0.0 0.9 %copy-start = (bf16[38,2048]{1,0:T(8,128)(2,1)S(1)}, bf16[38,2048]{1,0:T(8,128)(2,1)}, u32[]{:S(2)}) copy-start(bf16[38,2048]{1,0:T(8,128)(2,1)} %signal.1) | copy-start | bytes 466948
